TPU v7x, 128 devices: a whole 4x4x4 slice. The times are simulated.
128 devices in a mesh: dp: 8 (over x, core), expert: 16 (over y, z).
Axes of the slice: x: 4, y: 4, z: 4, core: 2. Of those that a mesh axis runs over, the one named last changes fastest.
Arguments:
- tokens: bfloat16 [32768, 4096], P(('dp', 'expert')), may hold values from -6 to 6
- cotangent: bfloat16 [32768, 4096], P(('dp', 'expert')), may hold values from -6 to 6
- routed_expert_index: int32 [32768, 2], P(('dp', 'expert')), may hold values from 0 to 15, all different within a row; in each aligned block of 256 rows (0 to 255, 256 to 511, ...) at most 40 rows name the same one
- router_gate_weights: float32 [32768, 2], P(('dp', 'expert')), may hold values from 0.05 to 1
- token_tenant_index: int32 [32768], P(('dp', 'expert')), may hold values from 0 to 7
- frozen_gate_weight: bfloat16 [16, 4096, 768], P('expert'), may hold values from -0.09375 to 0.09375
- frozen_up_weight: bfloat16 [16, 4096, 768], P('expert'), may hold values from -0.09375 to 0.09375
- frozen_down_weight: bfloat16 [16, 768, 4096], P('expert'), may hold values from -0.21875 to 0.21875
- adapter_down_matrices: bfloat16 [8, 16, 2, 16, 4096], P('dp', 'expert'), may hold values from -0.09375 to 0.09375
- adapter_up_matrices: bfloat16 [8, 16, 2, 16, 768], P('dp', 'expert'), may hold values from -1.5 to 1.5
Outputs:
- token_grads: bfloat16 [32768, 4096], P(('dp', 'expert'))
- down_grads: float32 [8, 16, 2, 16, 4096], P('dp', 'expert')
- up_grads: float32 [8, 16, 2, 16, 768], P('dp', 'expert')
Inputs may be any that keep to these rules, and one draw needn't show every extreme that they name: `routed_expert_index`: a token's 2 experts differ; at most 40 routes of the tokens of one device go to one expert, and some device sends exactly 40 to some expert.
All inputs are finite; a program needn't handle non-finite values.
Results may differ from a plain program's by a relative error of at most 0.0068.
Values may be sent and summed in bfloat16 or wider, within the bound.
No kernel may reach another device: no remote copies, remote signals or barrier semaphores. Data moves between devices by JAX's collectives and lax.ppermute only.
A program may use at most 192 MiB of HBM per device.

v0:
```python
import functools

import jax
import jax.numpy as jnp
from jax import lax
from jax.experimental import pallas as pl
from jax.experimental.pallas import tpu as pltpu
from jax.sharding import PartitionSpec as P

adapter_scale = 0.5
LANES = 128
CHUNKS = ((0, 24), (24, 40))
VMEM_BYTES = 56 * 1024 * 1024


def contract_last(left_side, right_side):
    return lax.dot_general(
        left_side, right_side, (((1,), (1,)), ((), ())), preferred_element_type=jnp.float32
    )


def contract_first(left_side, right_side):
    return lax.dot_general(
        left_side, right_side, (((0,), (0,)), ((), ())), preferred_element_type=jnp.float32
    )


def matmul(left_side, right_side):
    return jnp.dot(left_side, right_side, preferred_element_type=jnp.float32)


def route_slots(idx, experts):
    routes, tok_rows = idx.shape
    names = lax.broadcasted_iota(jnp.int32, (experts, tok_rows), 0)
    members = [(idx[k : k + 1, :] == names).astype(jnp.float32) for k in range(routes)]
    before = (
        lax.broadcasted_iota(jnp.int32, (tok_rows, tok_rows), 0)
        < lax.broadcasted_iota(jnp.int32, (tok_rows, tok_rows), 1)
    ).astype(jnp.bfloat16)
    running = matmul(sum(members).astype(jnp.bfloat16), before)
    return [jnp.sum(running * m, axis=0, keepdims=True).astype(jnp.int32) for m in members]


def slot_masks(idx, experts, low, high):
    routes, tok_rows = idx.shape
    size = high - low
    rows = lax.broadcasted_iota(jnp.int32, (experts * size, tok_rows), 0)
    masks = []
    for k, position in enumerate(route_slots(idx, experts)):
        inside = (position >= low) & (position < high)
        target = jnp.where(inside, idx[k : k + 1, :] * size + position - low, -1)
        masks.append(rows == target)
    return masks


def dispatch_kernel(experts, low, high, idx_ref, prob_ref, tenant_ref, tok_ref, cot_ref, out_ref):
    width = tok_ref.shape[1]
    masks = slot_masks(idx_ref[...], experts, low, high)
    weight = sum(
        jnp.sum(jnp.where(m, prob_ref[k : k + 1, :], 0.0), axis=1, keepdims=True)
        for k, m in enumerate(masks)
    )
    select = sum(m.astype(jnp.float32) for m in masks)
    tenant = jnp.sum(select * tenant_ref[...].astype(jnp.float32), axis=1, keepdims=True)
    out_ref[:, 2 * width :] = jnp.broadcast_to(tenant, (select.shape[0], LANES)).astype(
        jnp.bfloat16
    )
    select = select.astype(jnp.bfloat16)
    step = 512

    def body(i, carry):
        at = pl.multiple_of(i * step, step)
        out_ref[:, pl.ds(at, step)] = matmul(select, tok_ref[:, pl.ds(at, step)]).astype(
            jnp.bfloat16
        )
        out_ref[:, pl.ds(width + at, step)] = (
            matmul(select, cot_ref[:, pl.ds(at, step)]) * weight
        ).astype(jnp.bfloat16)
        return carry

    lax.fori_loop(0, width // step, body, 0)


def dispatch(idx, prob, tenant, tokens, cotangent, experts, low, high):
    tok_rows, width = tokens.shape
    rows = experts * (high - low)
    return pl.pallas_call(
        functools.partial(dispatch_kernel, experts, low, high),
        out_shape=jax.ShapeDtypeStruct((rows, 2 * width + LANES), jnp.bfloat16),
        in_specs=[pl.BlockSpec(memory_space=pltpu.VMEM)] * 5,
        out_specs=pl.BlockSpec(memory_space=pltpu.VMEM),
        compiler_params=pltpu.CompilerParams(vmem_limit_bytes=VMEM_BYTES),
        cost_estimate=pl.CostEstimate(
            flops=4 * rows * tok_rows * width,
            bytes_accessed=4 * tok_rows * width + 4 * rows * width,
            transcendentals=0,
        ),
        name="dispatch",
    )(idx, prob, tenant, tokens, cotangent)


def combine_kernel(experts, idx_ref, *refs):
    out_ref = refs[-1]
    total = None
    for (low, high), ret_ref in zip(CHUNKS, refs):
        masks = slot_masks(idx_ref[...], experts, low, high)
        select = sum(m.astype(jnp.float32) for m in masks).astype(jnp.bfloat16)
        part = contract_first(select, ret_ref[...])
        total = part if total is None else total + part
    out_ref[...] = total.astype(jnp.bfloat16)


def combine(idx, returned, experts):
    tok_rows, width = idx.shape[1], returned[0].shape[1]
    step = 1024
    rows = sum(r.shape[0] for r in returned)
    return pl.pallas_call(
        functools.partial(combine_kernel, experts),
        out_shape=jax.ShapeDtypeStruct((tok_rows, width), jnp.bfloat16),
        grid=(width // step,),
        in_specs=[pl.BlockSpec(idx.shape, lambda i: (0, 0))]
        + [pl.BlockSpec((r.shape[0], step), lambda i: (0, i)) for r in returned],
        out_specs=pl.BlockSpec((tok_rows, step), lambda i: (0, i)),
        compiler_params=pltpu.CompilerParams(vmem_limit_bytes=VMEM_BYTES),
        cost_estimate=pl.CostEstimate(
            flops=2 * rows * tok_rows * width,
            bytes_accessed=2 * (rows + tok_rows) * width,
            transcendentals=0,
        ),
        name="combine",
    )(idx, *returned)


def expert_chunk(received, gate_matrix, up_matrix, down_weight, down_gate, down_up, up_gate, up_up):
    width = gate_matrix.shape[0]
    groups = down_gate.shape[0]
    features = received[:, :width]
    routed = received[:, width : 2 * width]
    tenant = received[:, 2 * width : 2 * width + 1].astype(jnp.int32)
    rank = 16
    selector = (tenant == (jnp.arange(groups, dtype=jnp.int32) // rank)[None, :]).astype(
        jnp.float32
    )
    gate_low = (contract_last(features, down_gate) * selector).astype(jnp.bfloat16)
    up_low = (contract_last(features, down_up) * selector).astype(jnp.bfloat16)
    gate_pre = matmul(features, gate_matrix) + adapter_scale * matmul(gate_low, up_gate)
    up_pre = matmul(features, up_matrix) + adapter_scale * matmul(up_low, up_up)
    back = contract_last(routed, down_weight)
    sig = jax.nn.sigmoid(gate_pre)
    gate_grad = (back * up_pre * (sig + gate_pre * sig * (1.0 - sig))).astype(jnp.bfloat16)
    up_grad = (back * gate_pre * sig).astype(jnp.bfloat16)
    gate_back = (contract_last(gate_grad, up_gate) * selector).astype(jnp.bfloat16)
    up_back = (contract_last(up_grad, up_up) * selector).astype(jnp.bfloat16)
    total = contract_last(gate_grad, gate_matrix) + contract_last(up_grad, up_matrix)
    total = total + adapter_scale * (matmul(gate_back, down_gate) + matmul(up_back, down_up))
    down_part = (contract_first(gate_back, features), contract_first(up_back, features))
    up_part = (contract_first(gate_low, gate_grad), contract_first(up_low, up_grad))
    return total.astype(jnp.bfloat16), down_part, up_part


def reduce_to_owner(part):
    tenants = part.shape[0]
    me = lax.axis_index("dp")
    core, chip = me % 2, me // 2
    chips = tenants // 2
    pairs = part.reshape((chips, 2) + part.shape[1:])
    mine = lax.dynamic_index_in_dim(pairs, core, 1, keepdims=False)
    theirs = lax.dynamic_index_in_dim(pairs, 1 - core, 1, keepdims=False)
    mine = mine + lax.ppermute(theirs, "dp", [(i, i ^ 1) for i in range(tenants)])
    total = lax.dynamic_index_in_dim(mine, chip, 0, keepdims=False)
    for step in range(1, chips):
        sent = lax.dynamic_index_in_dim(mine, (chip + step) % chips, 0, keepdims=False)
        total = total + lax.ppermute(
            sent, "dp", [(i, (i + 2 * step) % tenants) for i in range(tenants)]
        )
    return total


def local(
    tokens,
    cotangent,
    routed_expert_index,
    router_gate_weights,
    token_tenant_index,
    frozen_gate_weight,
    frozen_up_weight,
    frozen_down_weight,
    adapter_down_matrices,
    adapter_up_matrices,
):
    experts = lax.axis_size("expert")
    tenants = lax.axis_size("dp")
    tok_rows, width = tokens.shape
    hidden = frozen_gate_weight.shape[2]
    rank = adapter_down_matrices.shape[3]
    idx = routed_expert_index.T
    prob = router_gate_weights.T
    tenant = token_tenant_index.reshape(1, tok_rows)
    adapters = jnp.concatenate([adapter_down_matrices[0, 0], adapter_up_matrices[0, 0]], axis=-1)
    held = lax.all_gather(adapters, "dp", axis=1, tiled=False)
    held = held.reshape(2, tenants * rank, width + hidden)
    down_gate, down_up = held[0, :, :width], held[1, :, :width]
    up_gate, up_up = held[0, :, width:], held[1, :, width:]
    returned, down_sum, up_sum = [], None, None
    for low, high in CHUNKS:
        sent = dispatch(idx, prob, tenant, tokens, cotangent, experts, low, high)
        received = lax.all_to_all(sent, "expert", split_axis=0, concat_axis=0, tiled=True)
        route_grad, down_part, up_part = expert_chunk(
            received,
            frozen_gate_weight[0],
            frozen_up_weight[0],
            frozen_down_weight[0],
            down_gate,
            down_up,
            up_gate,
            up_up,
        )
        returned.append(
            lax.all_to_all(route_grad, "expert", split_axis=0, concat_axis=0, tiled=True)
        )
        if down_sum is None:
            down_sum, up_sum = down_part, up_part
        else:
            down_sum = tuple(a + b for a, b in zip(down_sum, down_part))
            up_sum = tuple(a + b for a, b in zip(up_sum, up_part))
    down_sum = jnp.concatenate([d.reshape(tenants, rank, width) for d in down_sum], axis=1)
    up_sum = jnp.concatenate([u.reshape(tenants, rank, hidden) for u in up_sum], axis=1)
    owned = adapter_scale * reduce_to_owner(jnp.concatenate([down_sum, up_sum], axis=2))
    down_owned = owned[:, :width].reshape(1, 1, 2, rank, width)
    up_owned = owned[:, width:].reshape(1, 1, 2, rank, hidden)
    token_grads = combine(idx, returned, experts)
    return token_grads, down_owned, up_owned


def solution(mesh):
    in_specs = (
        P(("dp", "expert"), None),
        P(("dp", "expert"), None),
        P(("dp", "expert"), None),
        P(("dp", "expert"), None),
        P(("dp", "expert")),
        P("expert", None, None),
        P("expert", None, None),
        P("expert", None, None),
        P("dp", "expert", None, None, None),
        P("dp", "expert", None, None, None),
    )
    out_specs = (
        P(("dp", "expert"), None),
        P("dp", "expert", None, None, None),
        P("dp", "expert", None, None, None),
    )
    return jax.shard_map(local, mesh=mesh, in_specs=in_specs, out_specs=out_specs, check_vma=False)
```

profile of v0, /device:TPU:0, one launch (start us, length us, event | category | flops | bytes accessed | tf_op | source)
XLA Modules:
  0.0 315.8 jit_solution(9686591038083197996)
XLA Ops:
  7.2 7.0 %dispatch.3 = bf16[256,8320]{1,0:T(8,128)(2,1)} custom-call(s32[2,256]{1,0:T(2,128)} %bitcast.138, f32[2,256]{1,0:T(2,128)} %bitcast.141, s32[1,256]{1,0:T(1,128)} %bitcast.143, bf16[256,4096]{1,0:T(8,128)(2,1)} %tok_ref.3, bf16[256,4096]{1,0:T(8,128)(2,1)} %cot_ref.3), custom_call_target="tpu_custom_call" | custom-call | flops 1073741824 | bytes 8388608 | tf_op jit(solution)/shard_map/dispatch/pallas_call | solution.py:87
  14.2 8.3 %all-to-all-start.2 = ((bf16[16,16,8320]{2,1,0:T(8,128)(2,1)}), bf16[16,16,8320]{2,1,0:T(8,128)(2,1)}, u32[]{:S(2)}, u32[]{:S(2)}) async-start(bf16[16,16,8320]{2,1,0:T(8,128)(2,1)} %bitcast.122), calls=%async_computation.2 | async-start | bytes 8519680 | tf_op jit(solution)/shard_map/all_to_all | solution.py:207
  22.6 0.7 pad_maximum_fusion
  23.3 8.4 %dispatch.2 = bf16[384,8320]{1,0:T(8,128)(2,1)} custom-call(s32[2,256]{1,0:T(2,128)} %bitcast.139, f32[2,256]{1,0:T(2,128)} %bitcast.142, s32[1,256]{1,0:T(1,128)} %bitcast.144, bf16[256,4096]{1,0:T(8,128)(2,1)} %tok_ref.3, bf16[256,4096]{1,0:T(8,128)(2,1)} %cot_ref.3), custom_call_target="tpu_custom_call" | custom-call | flops 1610612736 | bytes 10485760 | tf_op jit(solution)/shard_map/dispatch/pallas_call | solution.py:87
  31.8 54.9 %all-to-all-done.2 = bf16[16,16,8320]{2,1,0:T(8,128)(2,1)} async-done(((bf16[16,16,8320]{2,1,0:T(8,128)(2,1)}), bf16[16,16,8320]{2,1,0:T(8,128)(2,1)}, u32[]{:S(2)}, u32[]{:S(2)}) %all-to-all-start.2) | async-done | bytes 4259872 | tf_op jit(solution)/shard_map/all_to_all | solution.py:207
  86.7 10.2 %all-to-all-start = ((bf16[16,24,8320]{2,1,0:T(8,128)(2,1)}), bf16[16,24,8320]{2,1,0:T(8,128)(2,1)}, u32[]{:S(2)}, u32[]{:S(2)}) async-start(bf16[16,24,8320]{2,1,0:T(8,128)(2,1)} %bitcast.119), calls=%async_computation | async-start | bytes 12779520 | tf_op jit(solution)/shard_map/all_to_all | solution.py:207
  96.9 1.0 convert_reduce_fusion.1
  97.9 5.2 %fusion.2 = f32[256,768]{1,0:T(8,128)S(1)} fusion(bf16[1,4096,768]{2,1,0:T(8,128)(2,1)} %param.15, bf16[256,8320]{1,0:T(8,128)(2,1)} %bitcast.17), kind=kOutput, calls=%fused_computation.2 | convolution fusion | flops 1610612736 | bytes 9175040 | tf_op jit(solution)/shard_map/dot_general | solution.py:29
  103.1 6.1 %fusion.10 = f32[256,768]{1,0:T(8,128)} fusion(bf16[1,4096,768]{2,1,0:T(8,128)(2,1)} %param.16, bf16[256,8320]{1,0:T(8,128)(2,1)} %bitcast.17), kind=kOutput, calls=%fused_computation.10 | convolution fusion | flops 1610612736 | bytes 9175040 | tf_op jit(solution)/shard_map/dot_general | solution.py:29
  109.2 2.7 fusion.63
  111.9 0.3 fusion.33
  112.2 2.5 fusion.62
  114.7 5.4 %multiply_convert_fusion.1 = (bf16[256,768]{1,0:T(8,128)(2,1)S(1)}, f32[256,768]{1,0:T(8,128)S(1)}) fusion(f32[256,768]{1,0:T(8,128)S(1)} %fusion.33, bf16[1,768,4096]{2,1,0:T(8,128)(2,1)} %param.17, bf16[256,8320]{1,0:T(8,128)(2,1)} %bitcast.17), kind=kOutput, calls=%fused_computation.85 | convolution fusion | flops 1611792384 | bytes 10354688 | tf_op jit(solution)/shard_map/dot_general | solution.py:17
  120.1 0.5 fusion.47
  120.6 0.3 fusion.64
  120.8 0.3 fusion.65
  121.1 0.7 fusion.72
  121.9 1.8 fusion
  123.7 0.4 slice-done.1
  124.2 1.9 fusion.22
  126.1 2.1 fusion.25
  128.2 52.4 %all-to-all-done = bf16[16,24,8320]{2,1,0:T(8,128)(2,1)} async-done(((bf16[16,24,8320]{2,1,0:T(8,128)(2,1)}), bf16[16,24,8320]{2,1,0:T(8,128)(2,1)}, u32[]{:S(2)}, u32[]{:S(2)}) %all-to-all-start) | async-done | bytes 6389792 | tf_op jit(solution)/shard_map/all_to_all | solution.py:207
  180.5 10.8 %all-to-all-start.3 = ((bf16[16,16,4096]{2,1,0:T(8,128)(2,1)}), bf16[16,16,4096]{2,1,0:T(8,128)(2,1)}, u32[]{:S(2)}, u32[]{:S(2)}) async-start(bf16[16,16,4096]{2,1,0:T(8,128)(2,1)} %bitcast.127), calls=%async_computation.3 | async-start | bytes 4194304 | tf_op jit(solution)/shard_map/all_to_all | solution.py:219
  191.3 1.0 convert_reduce_fusion
  192.3 6.5 %fusion.6 = f32[384,768]{1,0:T(8,128)S(1)} fusion(bf16[1,4096,768]{2,1,0:T(8,128)(2,1)} %param.15, bf16[384,8320]{1,0:T(8,128)(2,1)} %bitcast.4), kind=kOutput, calls=%fused_computation.6 | convolution fusion | flops 2415919104 | bytes 10616832 | tf_op jit(solution)/shard_map/dot_general | solution.py:29
  198.8 6.5 %fusion.14 = f32[384,768]{1,0:T(8,128)S(1)} fusion(bf16[1,4096,768]{2,1,0:T(8,128)(2,1)} %param.16, bf16[384,8320]{1,0:T(8,128)(2,1)} %bitcast.4), kind=kOutput, calls=%fused_computation.14 | convolution fusion | flops 2415919104 | bytes 10616832 | tf_op jit(solution)/shard_map/dot_general | solution.py:29
  205.3 2.9 fusion.54
  208.2 0.3 fusion.28
  208.5 4.6 %multiply_convert_fusion = (bf16[384,768]{1,0:T(8,128)(2,1)S(1)}, f32[384,768]{1,0:T(8,128)S(1)}) fusion(f32[384,768]{1,0:T(8,128)S(1)} %fusion.28, bf16[1,768,4096]{2,1,0:T(8,128)(2,1)S(1)} %bitcast.146, bf16[384,8320]{1,0:T(8,128)(2,1)} %bitcast.4), kind=kOutput, calls=%fused_computation.59 | convolution fusion | flops 2417688576 | bytes 12386304 | tf_op jit(solution)/shard_map/dot_general | solution.py:17
  213.1 3.0 fusion.57
  216.2 0.6 fusion.32
  216.8 0.3 fusion.77
  217.1 0.7 slice-done.9
  217.8 4.5 %fusion.4 = f32[384,4096]{1,0:T(8,128)} fusion(bf16[384,768]{1,0:T(8,128)(2,1)S(1)} %fusion.32, bf16[1,4096,768]{2,1,0:T(8,128)(2,1)S(1)} %bitcast.150), kind=kOutput, calls=%fused_computation.4 | convolution fusion | flops 2415919104 | bytes 13172736 | tf_op jit(solution)/shard_map/dot_general | solution.py:17
  222.3 0.3 fusion.78
  222.5 0.2 convolution_add_fusion.3
  222.8 0.2 convolution_add_fusion.4
  223.0 0.3 fusion.61
  223.4 2.6 fusion.37
  226.0 0.3 fusion.60
  226.3 2.6 fusion.39
  229.0 2.1 convolution_add_fusion.2
  231.1 2.1 convolution_add_fusion.1
  233.2 0.5 maximum_maximum_fusion
  233.7 1.6 dynamic-slice_bitcast_fusion
  235.3 1.0 fusion.73
  236.3 1.1 copy-done
  237.4 1.1 slice-done.2
  238.5 0.7 slice-done.3
  239.2 4.5 %fusion.12 = f32[384,4096]{1,0:T(8,128)} fusion(bf16[384,768]{1,0:T(8,128)(2,1)S(1)} %get-tuple-element.6, bf16[1,4096,768]{2,1,0:T(8,128)(2,1)S(1)} %bitcast.131), kind=kOutput, calls=%fused_computation.12 | convolution fusion | flops 2415919104 | bytes 13172736 | tf_op jit(solution)/shard_map/dot_general | solution.py:17
  243.7 7.5 %add_convert_fusion = bf16[384,4096]{1,0:T(8,128)(2,1)} fusion(f32[384,4096]{1,0:T(8,128)S(1)} %fusion.73, f32[384,4096]{1,0:T(8,128)} %fusion.4, f32[384,4096]{1,0:T(8,128)} %fusion.12, bf16[384,128]{1,0:T(8,128)(2,1)S(1)} %fusion.61, bf16[2,128,4864]{2,1,0:T(8,128)(2,1)S(1)} %copy-done.3), kind=kOutput, calls=%fused_computation.20 | convolution fusion | flops 410517504 | bytes 23166976 | tf_op jit(solution)/shard_map/dot_general | solution.py:29
  251.2 7.1 %all-to-all-start.1 = ((bf16[16,24,4096]{2,1,0:T(8,128)(2,1)}), bf16[16,24,4096]{2,1,0:T(8,128)(2,1)S(1)}, u32[]{:S(2)}, u32[]{:S(2)}) async-start(bf16[16,24,4096]{2,1,0:T(8,128)(2,1)} %bitcast.124), calls=%async_computation.1 | async-start | bytes 6291456 | tf_op jit(solution)/shard_map/all_to_all | solution.py:219
  258.5 2.7 bitcast_add_fusion
  261.2 1.5 copy-done.2
  262.7 1.3 dynamic-slice_bitcast_fusion.3
  264.0 1.5 collective-permute-start.1
  265.5 1.7 collective-permute-start.3
  267.2 0.3 collective-permute-start.2
  267.5 30.4 %all-to-all-done.1 = bf16[16,24,4096]{2,1,0:T(8,128)(2,1)S(1)} async-done(((bf16[16,24,4096]{2,1,0:T(8,128)(2,1)}), bf16[16,24,4096]{2,1,0:T(8,128)(2,1)S(1)}, u32[]{:S(2)}, u32[]{:S(2)}) %all-to-all-start.1) | async-done | bytes 3145760 | tf_op jit(solution)/shard_map/all_to_all | solution.py:219
  297.9 1.7 copy-done.1
  299.6 6.1 %combine.1 = bf16[256,4096]{1,0:T(8,128)(2,1)} custom-call(s32[2,256]{1,0:T(2,128)} %bitcast.140, bf16[384,4096]{1,0:T(8,128)(2,1)} %bitcast.123, bf16[256,4096]{1,0:T(8,128)(2,1)} %bitcast.19.refs_1_), custom_call_target="tpu_custom_call" | custom-call | flops 1342177280 | bytes 7340032 | tf_op jit(solution)/shard_map/combine/pallas_call | solution.py:117
  305.7 1.8 fusion.76
  307.5 0.6 slice.59
  308.2 0.8 slice.58
  (42 shorter events, 0.2 us)
Async XLA Ops:
  14.2 8.4 %copy-start.4 = (bf16[1,1,2,16,4096]{4,3,2,1,0:T(8,128)(2,1)S(1)}, bf16[1,1,2,16,4096]{4,3,2,1,0:T(8,128)(2,1)}, u32[]{:S(2)}) copy-start(bf16[1,1,2,16,4096]{4,3,2,1,0:T(8,128)(2,1)} %param.18) | copy-start | bytes 786436
  14.2 8.4 %copy-start.5 = (bf16[1,1,2,16,768]{4,3,2,1,0:T(8,128)(2,1)S(1)}, bf16[1,1,2,16,768]{4,3,2,1,0:T(8,128)(2,1)}, u32[]{:S(2)}) copy-start(bf16[1,1,2,16,768]{4,3,2,1,0:T(8,128)(2,1)} %param.19) | copy-start | bytes 147460
  14.2 72.5 %all-to-all-start.2 = ((bf16[16,16,8320]{2,1,0:T(8,128)(2,1)}), bf16[16,16,8320]{2,1,0:T(8,128)(2,1)}, u32[]{:S(2)}, u32[]{:S(2)}) async-start(bf16[16,16,8320]{2,1,0:T(8,128)(2,1)} %bitcast.122), calls=%async_computation.2 | async-start | bytes 8519680 | tf_op jit(solution)/shard_map/all_to_all | solution.py:207
  22.5 86.7 %all-gather.3.cloned.1.call-start = ((), (), s32[]{:S(2)}) async-start(), calls=%async_computation.4 | async-start | bytes 2801664 | tf_op jit(solution)/shard_map/all_gather | solution.py:200
  86.7 93.8 %all-to-all-start = ((bf16[16,24,8320]{2,1,0:T(8,128)(2,1)}), bf16[16,24,8320]{2,1,0:T(8,128)(2,1)}, u32[]{:S(2)}, u32[]{:S(2)}) async-start(bf16[16,24,8320]{2,1,0:T(8,128)(2,1)} %bitcast.119), calls=%async_computation | async-start | bytes 12779520 | tf_op jit(solution)/shard_map/all_to_all | solution.py:207
  109.2 2.7 copy-start.3
  112.2 9.7 %slice-start.6 = ((s8[6291456]{0:T(1024)(128)(4,1)}), s8[4194304]{0:T(1024)(128)(4,1)S(1)}, s32[]{:S(2)}) async-start(s8[6291456]{0:T(1024)(128)(4,1)} %bitcast.147), calls=%async_computation.11 | async-start | bytes 8388608
  114.6 5.5 %copy-start.6 = (f32[256,768]{1,0:T(8,128)S(1)}, f32[256,768]{1,0:T(8,128)}, u32[]{:S(2)}) copy-start(f32[256,768]{1,0:T(8,128)} %fusion.10) | copy-start | bytes 2359300
  114.7 7.2 %slice-start.7 = ((s8[6291456]{0:T(1024)(128)(4,1)}), s8[2097152]{0:T(1024)(128)(4,1)S(1)}, s32[]{:S(2)}) async-start(s8[6291456]{0:T(1024)(128)(4,1)} %bitcast.147), calls=%async_computation.12 | async-start | bytes 4194304
  121.1 2.6 slice-start
  121.8 2.3 slice-start.1
  180.5 70.7 %all-to-all-start.3 = ((bf16[16,16,4096]{2,1,0:T(8,128)(2,1)}), bf16[16,16,4096]{2,1,0:T(8,128)(2,1)}, u32[]{:S(2)}, u32[]{:S(2)}) async-start(bf16[16,16,4096]{2,1,0:T(8,128)(2,1)} %bitcast.127), calls=%async_computation.3 | async-start | bytes 4194304 | tf_op jit(solution)/shard_map/all_to_all | solution.py:219
  192.3 16.2 %slice-start.4 = ((s8[6291456]{0:T(1024)(128)(4,1)}), s8[4194304]{0:T(1024)(128)(4,1)S(1)}, s32[]{:S(2)}) async-start(s8[6291456]{0:T(1024)(128)(4,1)} %bitcast.145), calls=%async_computation.9 | async-start | bytes 8388608
  198.8 9.7 %slice-start.5 = ((s8[6291456]{0:T(1024)(128)(4,1)}), s8[2097152]{0:T(1024)(128)(4,1)S(1)}, s32[]{:S(2)}) async-start(s8[6291456]{0:T(1024)(128)(4,1)} %bitcast.145), calls=%async_computation.10 | async-start | bytes 4194304
  213.1 4.0 %slice-start.8 = ((s8[6291456]{0:T(1024)(128)(4,1)}), s8[4194304]{0:T(1024)(128)(4,1)S(1)}, s32[]{:S(2)}) async-start(s8[6291456]{0:T(1024)(128)(4,1)} %bitcast.149), calls=%async_computation.13 | async-start | bytes 8388608
  216.2 1.6 slice-start.9
  233.7 3.7 %copy-start = (f32[8,32,4864]{2,1,0:T(8,128)}, f32[8,32,4864]{2,1,0:T(8,128)S(1)}, u32[]{:S(2)}) copy-start(f32[8,32,4864]{2,1,0:T(8,128)S(1)} %maximum_maximum_fusion) | copy-start | bytes 14942212
  233.7 4.8 %slice-start.2 = ((s8[6291456]{0:T(1024)(128)(4,1)}), s8[4194304]{0:T(1024)(128)(4,1)S(1)}, s32[]{:S(2)}) async-start(s8[6291456]{0:T(1024)(128)(4,1)} %bitcast.130), calls=%async_computation.7 | async-start | bytes 8388608
  235.3 3.8 %slice-start.3 = ((s8[6291456]{0:T(1024)(128)(4,1)}), s8[2097152]{0:T(1024)(128)(4,1)S(1)}, s32[]{:S(2)}) async-start(s8[6291456]{0:T(1024)(128)(4,1)} %bitcast.130), calls=%async_computation.8 | async-start | bytes 4194304
  235.3 23.1 %collective-permute-start = (f32[4,32,4864]{2,1,0:T(8,128)}, f32[4,32,4864]{2,1,0:T(8,128)}, u32[]{:S(2)}, u32[]{:S(2)}) collective-permute-start(f32[4,32,4864]{2,1,0:T(8,128)} %dynamic-slice_bitcast_fusion), channel_id=1, source_target_pairs={{0,16},{16,0},{32,48},{48,32},{64,80},{80,64},{96,112},{112,96},{1... | collective-permute-start | bytes 7471112 | tf_op jit(solution)/shard_map/ppermute | solution.py:169
  251.2 46.7 %all-to-all-start.1 = ((bf16[16,24,4096]{2,1,0:T(8,128)(2,1)}), bf16[16,24,4096]{2,1,0:T(8,128)(2,1)S(1)}, u32[]{:S(2)}, u32[]{:S(2)}) async-start(bf16[16,24,4096]{2,1,0:T(8,128)(2,1)} %bitcast.124), calls=%async_computation.1 | async-start | bytes 6291456 | tf_op jit(solution)/shard_map/all_to_all | solution.py:219
  261.2 1.5 copy-start.2
  264.0 41.8 %collective-permute-start.1 = (f32[32,4864]{1,0:T(8,128)}, f32[32,4864]{1,0:T(8,128)}, u32[]{:S(2)}, u32[]{:S(2)}) collective-permute-start(f32[32,4864]{1,0:T(8,128)} %get-tuple-element.3), channel_id=1, source_target_pairs={{0,32},{16,48},{32,64},{48,80},{64,96},{80,112},{96,0},{112,16},{1... | collective-permute-start | bytes 1867784 | tf_op jit(solution)/shard_map/ppermute | solution.py:173
  265.5 40.3 %collective-permute-start.3 = (f32[32,4864]{1,0:T(8,128)}, f32[32,4864]{1,0:T(8,128)}, u32[]{:S(2)}, u32[]{:S(2)}) collective-permute-start(f32[32,4864]{1,0:T(8,128)} %get-tuple-element.4), channel_id=1, source_target_pairs={{0,96},{16,112},{32,0},{48,16},{64,32},{80,48},{96,64},{112,80},{1... | collective-permute-start | bytes 1867784 | tf_op jit(solution)/shard_map/ppermute | solution.py:173
  267.2 38.5 %collective-permute-start.2 = (f32[32,4864]{1,0:T(8,128)}, f32[32,4864]{1,0:T(8,128)}, u32[]{:S(2)}, u32[]{:S(2)}) collective-permute-start(f32[32,4864]{1,0:T(8,128)} %get-tuple-element.5), channel_id=1, source_target_pairs={{0,64},{16,80},{32,96},{48,112},{64,0},{80,16},{96,32},{112,48},{1... | collective-permute-start | bytes 1867784 | tf_op jit(solution)/shard_map/ppermute | solution.py:173
  297.9 1.7 copy-start.1
Sparse Core Ops, SparseCore 0:
  25.6 27.3 all-gather.2
where the time goes:
time: 317 us; the launch traced here: 316 us
  waiting for transfers between devices  138 us (44%)
  matrix products  82.7 us (26%)
  starting transfers between devices  40 us (13%)
  Pallas kernels  21.6 us (7%)
  between operations  14.6 us (5%)
  local copies, waits for them, and re-layouts  11.5 us (4%)
  other arithmetic  7.68 us (2%)
    all_to_all x2, waiting for transfers between devices, local(): lax.all_to_all(sent, 'expert', split_axis=0, concat_axis=0, tiled=True)  107 us
    dot_general x12, matrix products, matmul(): return jnp.dot(left_side, right_side, preferred_element_type=jnp.float32)  37.2 us
    dot_general x14, matrix products, contract_last(): lax.dot_general(left_side, right_side, (((1,), (1,)), ((), ())), preferre...  35 us
    all_to_all x2, waiting for transfers between devices, local(): lax.all_to_all(route_grad, 'expert', split_axis=0, concat_axis=0, tiled=T...  30.4 us
    all_to_all x2, starting transfers between devices, local(): lax.all_to_all(sent, 'expert', split_axis=0, concat_axis=0, tiled=True)  18.5 us
    all_to_all x2, starting transfers between devices, local(): lax.all_to_all(route_grad, 'expert', split_axis=0, concat_axis=0, tiled=T...  17.9 us
    pallas_call x2, Pallas kernels, dispatch(): pl.pallas_call(functools.partial(dispatch_kernel, experts, low, high), ou...  15.5 us
    dot_general x8, matrix products, contract_first(): lax.dot_general(left_side, right_side, (((0,), (0,)), ((), ())), preferre...  10.5 us
  transfers between devices with their start and end apart: 9, of which 3 were waited for; matrix products, arithmetic and copies ran while one was open for 29% of the time, Pallas kernels for 5%

commit v1 on v0

v1 whole, which is shorter than its diff:
```python
import functools

import jax
import jax.numpy as jnp
from jax import lax
from jax.experimental import pallas as pl
from jax.experimental.pallas import tpu as pltpu
from jax.sharding import PartitionSpec as P

adapter_scale = 0.5
LANES = 128
VMEM_BYTES = 60 * 1024 * 1024


def contract_last(left_side, right_side):
    return lax.dot_general(
        left_side, right_side, (((1,), (1,)), ((), ())), preferred_element_type=jnp.float32
    )


def matmul(left_side, right_side):
    return jnp.dot(left_side, right_side, preferred_element_type=jnp.float32)


def slot_masks(idx, experts, capacity):
    routes, tok_rows = idx.shape
    names = lax.broadcasted_iota(jnp.int32, (experts, tok_rows), 0)
    members = [(idx[k : k + 1, :] == names).astype(jnp.float32) for k in range(routes)]
    before = (
        lax.broadcasted_iota(jnp.int32, (tok_rows, tok_rows), 0)
        < lax.broadcasted_iota(jnp.int32, (tok_rows, tok_rows), 1)
    ).astype(jnp.bfloat16)
    running = matmul(sum(members).astype(jnp.bfloat16), before)
    rows = lax.broadcasted_iota(jnp.int32, (experts * capacity, tok_rows), 0)
    masks = []
    for k, member in enumerate(members):
        position = jnp.sum(running * member, axis=0, keepdims=True).astype(jnp.int32)
        masks.append(rows == idx[k : k + 1, :] * capacity + position)
    return masks


def dispatch_kernel(
    experts,
    capacity,
    idx_ref,
    prob_ref,
    tenant_ref,
    tok_ref,
    cot_ref,
    out_ref,
    select,
    weight,
    tenant_rows,
    feat_out,
    cot_out,
    sems,
    tenant_sem,
):
    step = pl.program_id(0)
    steps = pl.num_programs(0)
    block = tok_ref.shape[1]
    width = block * steps
    slot = lax.rem(step, 2)

    def copies(at, slot):
        column = pl.multiple_of(at * block, block)
        return (
            pltpu.make_async_copy(
                feat_out.at[slot], out_ref.at[:, pl.ds(column, block)], sems.at[0, slot]
            ),
            pltpu.make_async_copy(
                cot_out.at[slot], out_ref.at[:, pl.ds(width + column, block)], sems.at[1, slot]
            ),
        )

    tenant_copy = pltpu.make_async_copy(
        tenant_rows, out_ref.at[:, pl.ds(2 * width, LANES)], tenant_sem
    )

    @pl.when(step == 0)
    def _():
        masks = slot_masks(idx_ref[...], experts, capacity)
        filled = sum(m.astype(jnp.float32) for m in masks)
        weight[...] = sum(
            jnp.sum(jnp.where(m, prob_ref[k : k + 1, :], 0.0), axis=1, keepdims=True)
            for k, m in enumerate(masks)
        )
        tenant = jnp.sum(filled * tenant_ref[...].astype(jnp.float32), axis=1, keepdims=True)
        tenant_rows[...] = jnp.broadcast_to(tenant, tenant_rows.shape).astype(jnp.bfloat16)
        tenant_copy.start()
        select[...] = filled.astype(jnp.bfloat16)

    @pl.when(step >= 2)
    def _():
        for copy in copies(step - 2, slot):
            copy.wait()

    feat_out[slot] = matmul(select[...], tok_ref[...]).astype(jnp.bfloat16)
    cot_out[slot] = (matmul(select[...], cot_ref[...]) * weight[...]).astype(jnp.bfloat16)
    for copy in copies(step, slot):
        copy.start()

    @pl.when(step == steps - 1)
    def _():
        for copy in copies(step - 1, 1 - slot):
            copy.wait()
        for copy in copies(step, slot):
            copy.wait()
        tenant_copy.wait()


def dispatch(idx, prob, tenant, tokens, cotangent, experts, capacity):
    tok_rows, width = tokens.shape
    rows = experts * capacity
    block = 512
    return pl.pallas_call(
        functools.partial(dispatch_kernel, experts, capacity),
        out_shape=jax.ShapeDtypeStruct((rows, 2 * width + LANES), jnp.bfloat16),
        grid=(width // block,),
        in_specs=[
            pl.BlockSpec(idx.shape, lambda i: (0, 0)),
            pl.BlockSpec(prob.shape, lambda i: (0, 0)),
            pl.BlockSpec(tenant.shape, lambda i: (0, 0)),
            pl.BlockSpec((tok_rows, block), lambda i: (0, i)),
            pl.BlockSpec((tok_rows, block), lambda i: (0, i)),
        ],
        out_specs=pl.BlockSpec(memory_space=pl.ANY),
        scratch_shapes=[
            pltpu.VMEM((rows, tok_rows), jnp.bfloat16),
            pltpu.VMEM((rows, 1), jnp.float32),
            pltpu.VMEM((rows, LANES), jnp.bfloat16),
            pltpu.VMEM((2, rows, block), jnp.bfloat16),
            pltpu.VMEM((2, rows, block), jnp.bfloat16),
            pltpu.SemaphoreType.DMA((2, 2)),
            pltpu.SemaphoreType.DMA,
        ],
        compiler_params=pltpu.CompilerParams(vmem_limit_bytes=VMEM_BYTES),
        cost_estimate=pl.CostEstimate(
            flops=4 * rows * tok_rows * width,
            bytes_accessed=4 * tok_rows * width + 4 * rows * width,
            transcendentals=0,
        ),
        name="dispatch",
    )(idx, prob, tenant, tokens, cotangent)


def combine_kernel(experts, capacity, idx_ref, ret_ref, out_ref, select):
    @pl.when(pl.program_id(0) == 0)
    def _():
        filled = sum(m.astype(jnp.float32) for m in slot_masks(idx_ref[...], experts, capacity))
        select[...] = filled.T.astype(jnp.bfloat16)

    out_ref[...] = matmul(select[...], ret_ref[...]).astype(jnp.bfloat16)


def combine(idx, returned, experts, capacity):
    tok_rows, width = idx.shape[1], returned.shape[1]
    block = 512
    rows = returned.shape[0]
    return pl.pallas_call(
        functools.partial(combine_kernel, experts, capacity),
        out_shape=jax.ShapeDtypeStruct((tok_rows, width), jnp.bfloat16),
        grid=(width // block,),
        in_specs=[
            pl.BlockSpec(idx.shape, lambda i: (0, 0)),
            pl.BlockSpec((rows, block), lambda i: (0, i)),
        ],
        out_specs=pl.BlockSpec((tok_rows, block), lambda i: (0, i)),
        scratch_shapes=[pltpu.VMEM((tok_rows, rows), jnp.bfloat16)],
        compiler_params=pltpu.CompilerParams(vmem_limit_bytes=VMEM_BYTES),
        cost_estimate=pl.CostEstimate(
            flops=2 * rows * tok_rows * width,
            bytes_accessed=2 * (rows + tok_rows) * width,
            transcendentals=0,
        ),
        name="combine",
    )(idx, returned)


def expert_kernel(
    rank,
    got_ref,
    held_ref,
    gate_ref,
    up_ref,
    down_ref,
    route_out,
    part_out,
    feat,
    cot,
    tenant,
    low_held,
    high_held,
    gate,
    up,
    down,
    grads,
    down_sum,
    up_sum,
    gate_pre,
    up_pre,
    sems,
    out_sems,
):
    width = feat.shape[1]
    hidden = down.shape[0]
    groups = held_ref.shape[0]
    block = 256
    step = 512
    parts = hidden // block

    stages = (
        (
            (got_ref.at[:, pl.ds(2 * width, LANES)], tenant),
            (got_ref.at[:, pl.ds(0, width)], feat),
            (held_ref.at[:, pl.ds(0, width)], low_held),
        ),
        ((gate_ref, gate), (held_ref.at[:, pl.ds(width, hidden)], high_held)),
        ((up_ref, up),),
        ((got_ref.at[:, pl.ds(width, width)], cot), (down_ref, down)),
    )
    copies = []
    for stage in stages:
        first = sum(len(c) for c in copies)
        copies.append(
            [
                pltpu.make_async_copy(source, target, sems.at[first + i])
                for i, (source, target) in enumerate(stage)
            ]
        )
    ahead = 2
    for stage in copies[:ahead]:
        for copy in stage:
            copy.start()

    def arrive(i):
        for copy in copies[i]:
            copy.wait()
        if i + ahead < len(copies):
            for copy in copies[i + ahead]:
                copy.start()

    arrive(0)
    owner = lax.broadcasted_iota(jnp.int32, (1, groups), 1) // (2 * rank)
    selector = (tenant[:, 0:1].astype(jnp.int32) == owner).astype(jnp.float32)
    low = (contract_last(feat[...], low_held[...]) * selector).astype(jnp.bfloat16)
    arrive(1)
    is_gate = lax.broadcasted_iota(jnp.int32, (groups, 1), 0) // rank % 2 == 0
    high = high_held[...].astype(jnp.float32)
    high_gate = jnp.where(is_gate, high, 0.0).astype(jnp.bfloat16)
    high_up = jnp.where(is_gate, 0.0, high).astype(jnp.bfloat16)
    for h in range(parts):
        at = slice(h * block, (h + 1) * block)
        gate_pre[:, at] = matmul(feat[...], gate[:, at]) + adapter_scale * matmul(
            low, high_gate[:, at]
        )
    arrive(2)
    for h in range(parts):
        at = slice(h * block, (h + 1) * block)
        up_pre[:, at] = matmul(feat[...], up[:, at]) + adapter_scale * matmul(low, high_up[:, at])
    arrive(3)
    for h in range(parts):
        at = slice(h * block, (h + 1) * block)
        after = slice(hidden + h * block, hidden + (h + 1) * block)
        back = contract_last(cot[...], down[at])
        pre = gate_pre[:, at]
        sig = jax.nn.sigmoid(pre)
        grads[:, at] = (back * up_pre[:, at] * (sig + pre * sig * (1.0 - sig))).astype(jnp.bfloat16)
        grads[:, after] = (back * pre * sig).astype(jnp.bfloat16)
    low_back = contract_last(grads[:, :hidden], high_gate) + contract_last(
        grads[:, hidden:], high_up
    )
    low_back = (low_back * selector).astype(jnp.bfloat16)
    back_t = low_back.astype(jnp.float32).T.astype(jnp.bfloat16)
    low_t = low.astype(jnp.float32).T.astype(jnp.bfloat16)
    up_sum[...] = adapter_scale * jnp.where(
        is_gate, matmul(low_t, grads[:, :hidden]), matmul(low_t, grads[:, hidden:])
    )
    leaving = [
        pltpu.make_async_copy(up_sum, part_out.at[:, pl.ds(width, hidden)], out_sems.at[0])
    ]
    leaving[-1].start()
    for i in range(width // step):
        at = pl.ds(i * step, step)
        down_sum[:, at] = adapter_scale * matmul(back_t, feat[:, at])
        leaving.append(
            pltpu.make_async_copy(down_sum.at[:, at], part_out.at[:, at], out_sems.at[len(leaving)])
        )
        leaving[-1].start()
    for i in range(width // step):
        at = pl.ds(i * step, step)
        cot[:, at] = (
            contract_last(grads[:, :hidden], gate[at])
            + contract_last(grads[:, hidden:], up[at])
            + adapter_scale * matmul(low_back, low_held[:, at])
        ).astype(jnp.bfloat16)
        leaving.append(
            pltpu.make_async_copy(cot.at[:, at], route_out.at[:, at], out_sems.at[len(leaving)])
        )
        leaving[-1].start()
    for copy in leaving:
        copy.wait()


def expert_pass(received, held, gate_matrix, up_matrix, down_weight, rank):
    rows = received.shape[0]
    width, hidden = gate_matrix.shape
    groups = held.shape[0]
    anywhere = pl.BlockSpec(memory_space=pl.ANY)
    return pl.pallas_call(
        functools.partial(expert_kernel, rank),
        out_shape=(
            jax.ShapeDtypeStruct((rows, width), jnp.bfloat16),
            jax.ShapeDtypeStruct((groups, width + hidden), jnp.float32),
        ),
        in_specs=[anywhere] * 5,
        out_specs=(anywhere, anywhere),
        scratch_shapes=[
            pltpu.VMEM((rows, width), jnp.bfloat16),
            pltpu.VMEM((rows, width), jnp.bfloat16),
            pltpu.VMEM((rows, LANES), jnp.bfloat16),
            pltpu.VMEM((groups, width), jnp.bfloat16),
            pltpu.VMEM((groups, hidden), jnp.bfloat16),
            pltpu.VMEM((width, hidden), jnp.bfloat16),
            pltpu.VMEM((width, hidden), jnp.bfloat16),
            pltpu.VMEM((hidden, width), jnp.bfloat16),
            pltpu.VMEM((rows, 2 * hidden), jnp.bfloat16),
            pltpu.VMEM((groups, width), jnp.float32),
            pltpu.VMEM((groups, hidden), jnp.float32),
            pltpu.VMEM((rows, hidden), jnp.float32),
            pltpu.VMEM((rows, hidden), jnp.float32),
            pltpu.SemaphoreType.DMA((8,)),
            pltpu.SemaphoreType.DMA((1 + 2 * (width // 512),)),
        ],
        compiler_params=pltpu.CompilerParams(vmem_limit_bytes=VMEM_BYTES),
        cost_estimate=pl.CostEstimate(
            flops=10 * rows * width * hidden + 6 * rows * width * groups,
            bytes_accessed=6 * width * hidden + 6 * rows * width,
            transcendentals=rows * hidden,
        ),
        name="expert_pass",
    )(received, held, gate_matrix, up_matrix, down_weight)


def chip_sums(part):
    chips = part.shape[0]
    devices = lax.axis_size("dp")
    per_chip = devices // chips
    chip = lax.axis_index("dp") // per_chip
    own = lax.dynamic_index_in_dim(part, chip, 0, keepdims=False)
    arrived = []
    for step in range(1, chips):
        sent = lax.dynamic_index_in_dim(part, (chip + step) % chips, 0, keepdims=False)
        arrived.append(
            lax.ppermute(
                sent, "dp", [(i, (i + per_chip * step) % devices) for i in range(devices)]
            )
        )
    return own, arrived


def exchange(named, rows):
    return lax.cond(
        named,
        lambda r: lax.all_to_all(r, "expert", split_axis=0, concat_axis=0, tiled=True),
        jnp.zeros_like,
        rows,
    )


def local(
    tokens,
    cotangent,
    routed_expert_index,
    router_gate_weights,
    token_tenant_index,
    frozen_gate_weight,
    frozen_up_weight,
    frozen_down_weight,
    adapter_down_matrices,
    adapter_up_matrices,
):
    experts = lax.axis_size("expert")
    tenants = lax.axis_size("dp")
    tok_rows, width = tokens.shape
    routes = routed_expert_index.shape[1]
    hidden = frozen_gate_weight.shape[2]
    rank = adapter_down_matrices.shape[3]
    groups = tenants * rank
    capacity = 5 * tok_rows * routes // (4 * experts)
    idx = routed_expert_index.T
    prob = router_gate_weights.T
    tenant = token_tenant_index.reshape(1, tok_rows)
    adapters = jnp.concatenate([adapter_down_matrices[0, 0], adapter_up_matrices[0, 0]], axis=-1)
    held = lax.all_gather(adapters, "dp", axis=0, tiled=True)
    sent = dispatch(idx, prob, tenant, tokens, cotangent, experts, capacity)
    named = routed_expert_index[0, 0] >= 0
    received = exchange(named, sent)
    received, held = lax.optimization_barrier((received, held))
    route_grad, part = expert_pass(
        received,
        held.reshape(2 * groups, width + hidden),
        frozen_gate_weight[0],
        frozen_up_weight[0],
        frozen_down_weight[0],
        rank,
    )
    own, arrived = chip_sums(part.reshape(tenants // 2, 4 * rank, width + hidden))
    returned = exchange(named, route_grad)
    returned, own, *arrived = lax.optimization_barrier((returned, own, *arrived))
    token_grads = combine(idx, returned, experts, capacity)
    total = sum(arrived, own).reshape(2, 2 * rank, width + hidden)
    core = lax.axis_index("dp") % 2
    theirs = lax.dynamic_index_in_dim(total, 1 - core, 0, keepdims=False)
    owned = lax.dynamic_index_in_dim(total, core, 0, keepdims=False) + lax.ppermute(
        theirs, "dp", [(i, i ^ 1) for i in range(tenants)]
    )
    down_owned = owned[:, :width].reshape(1, 1, 2, rank, width)
    up_owned = owned[:, width:].reshape(1, 1, 2, rank, hidden)
    return token_grads, down_owned, up_owned


def solution(mesh):
    in_specs = (
        P(("dp", "expert"), None),
        P(("dp", "expert"), None),
        P(("dp", "expert"), None),
        P(("dp", "expert"), None),
        P(("dp", "expert")),
        P("expert", None, None),
        P("expert", None, None),
        P("expert", None, None),
        P("dp", "expert", None, None, None),
        P("dp", "expert", None, None, None),
    )
    out_specs = (
        P(("dp", "expert"), None),
        P("dp", "expert", None, None, None),
        P("dp", "expert", None, None, None),
    )
    return jax.shard_map(local, mesh=mesh, in_specs=in_specs, out_specs=out_specs, check_vma=False)
```

time: 317 us -> 284 us (0.90)
  blocking collectives: 0 us -> 194 us
  waiting for transfers between devices: 138 us -> 0.03 us
  matrix products: 82.7 us -> 0 us
  starting transfers between devices: 40 us -> 5.77 us
  Pallas kernels: 21.6 us -> 54.9 us
  other arithmetic: 7.68 us -> 4.05 us
  local copies, waits for them, and re-layouts: 11.5 us -> 8.2 us
    all_to_all x0 -> x2, blocking collectives: none -> 194 us  [exchange(): lax.all_to_all(r, 'expert', split_axis=0, concat_axis=0, tiled=True)]
    all_to_all x4 -> x0, waiting for transfers between devices: 138 us -> none  [the longest x2 107 us: local(): lax.all_to_all(sent, 'expert', split_axis=0, concat_axis=0, tiled=True)]
    dot_general x34 -> x0, matrix products: 82.7 us -> none  [the longest x12 37.2 us: matmul(): return jnp.dot(left_side, right_side, preferred_element_type=jnp.float32)]
    all_to_all x4 -> x0, starting transfers between devices: 36.4 us -> none  [the longest x2 18.5 us: local(): lax.all_to_all(sent, 'expert', split_axis=0, concat_axis=0, tiled=True)]
    pallas_call x3, Pallas kernels: 21.6 us -> 54.9 us  [the longest x1 37.2 us: expert_pass(): pl.pallas_call(functools.partial(expert_kernel, rank), out_shape=(jax.Sha...]
    unnamed x34 -> x2, local copies, waits for them, and re-layouts: 7.17 us -> 1.07 us
  transfers between devices with their start and end apart: 9 -> 5, of which waited for: 3 -> 0; matrix products, arithmetic and copies ran while one was open for 29% -> 0% of each run, Pallas kernels for 5% -> 6%
where the time goes in v1:
time: 284 us; the launch traced here: 282 us
  blocking collectives  194 us (68%)
  Pallas kernels  54.9 us (19%)
  between operations  14.8 us (5%)
  local copies, waits for them, and re-layouts  8.2 us (3%)
  starting transfers between devices  5.77 us (2%)
  other arithmetic  4.05 us (1%)
    all_to_all x2, blocking collectives, exchange(): lax.all_to_all(r, 'expert', split_axis=0, concat_axis=0, tiled=True)  194 us
    pallas_call x1, Pallas kernels, expert_pass(): pl.pallas_call(functools.partial(expert_kernel, rank), out_shape=(jax.Sha...  37.2 us
    pallas_call x1, Pallas kernels, dispatch(): pl.pallas_call(functools.partial(dispatch_kernel, experts, capacity), out...  9.64 us
    pallas_call x1, Pallas kernels, combine(): pl.pallas_call(functools.partial(combine_kernel, experts, capacity), out_...  7.99 us
  transfers between devices with their start and end apart: 5, of which 0 were waited for; matrix products, arithmetic and copies ran while one was open for 0% of the time, Pallas kernels for 6%

profile of v1, /device:TPU:0, one launch (start us, length us, event | category | flops | bytes accessed | tf_op | source)
XLA Modules:
  0.0 282.1 jit_solution(2418656061673107720)
XLA Ops:
  7.2 0.0 all-gather.2.cloned.1.call-start
  7.2 1.7 pad_maximum_fusion
  8.9 0.0 all-gather.2.cloned.1.call-update
  9.0 1.2 slice.9
  10.9 9.6 %dispatch.1 = bf16[640,8320]{1,0:T(8,128)(2,1)} custom-call(s32[2,256]{1,0:T(2,128)} %bitcast.41, f32[2,256]{1,0:T(2,128)} %bitcast.43, s32[1,256]{1,0:T(1,128)} %bitcast.44, bf16[256,4096]{1,0:T(8,128)(2,1)} %tok_ref.1, bf16[256,4096]{1,0:T(8,128)(2,1)} %cot_ref.1), custom_call_target="tpu_custom_call" | custom-call | flops 2684354560 | bytes 14680064 | tf_op jit(solution)/shard_map/dispatch/pallas_call | solution.py:116
  20.5 129.7 %conditional.2 = (bf16[640,8320]{1,0:T(8,128)(2,1)}) conditional(s32[]{:T(128)} %bitcast.5, () %tuple.23, bf16[640,8320]{1,0:T(8,128)(2,1)} %dispatch.1), branch_computations={%region_0.0_spmd, %region_1.0_spmd} | conditional | bytes 21299208 | solution.py:363
  20.6 129.7 %all_to_all.18 = bf16[16,40,8320]{2,1,0:T(8,128)(2,1)} all-to-all(bf16[16,40,8320]{2,1,0:T(8,128)(2,1)} %bitcast.30), channel_id=1, replica_groups=mesh['dp'=8,'expert'=16] {'expert'}, dimensions={0} | all-to-all | bytes 21299200 | tf_op jit(solution)/shard_map/cond/branch_1_fun/all_to_all | solution.py:365
  150.2 0.0 all-gather.2.cloned.1.call-done
  150.2 37.2 %expert_pass.1 = (bf16[640,4096]{1,0:T(8,128)(2,1)}, f32[256,4864]{1,0:T(8,128)}) custom-call(bf16[640,8320]{1,0:T(8,128)(2,1)} %get-tuple-element.33.got_ref, bf16[256,4864]{1,0:T(8,128)(2,1)} %bitcast.48, bf16[4096,768]{1,0:T(8,128)(2,1)} %bitcast.45, bf16[4096,768]{1,0:T(8,128)(2,1)} %bitcast.46, bf16[768,4096]{1,0:T(8,128)(2,1)} %bitcast.47), custom_call_target="tpu_custom_call" | custom-call | flops 24159191040 | bytes 34603008 | tf_op jit(solution)/shard_map/expert_pass/pallas_call | solution.py:310
  187.5 4.4 %dynamic-slice_bitcast_fusion = (f32[64,4864]{1,0:T(8,128)}, f32[64,4864]{1,0:T(8,128)}, f32[64,4864]{1,0:T(8,128)}, f32[64,4864]{1,0:T(8,128)S(1)}) fusion(f32[4,64,4864]{2,1,0:T(8,128)} %bitcast.36, s32[]{:T(128)S(6)} %select_n.50, s32[]{:T(128)S(6)} %select_n.48, s32[]{:T(128)S(6)} %select_n.46, s32[]{:T(128)S(6)} %select_n.44), kind=kLoop, calls=%fused_computation.1 | loop fusion | bytes 9961488 | tf_op jit(solution)/shard_map/jit(dynamic_index_in_dim)/squeeze | solution.py:353
  191.9 1.5 collective-permute-start
  193.4 2.7 collective-permute-start.1
  196.1 1.4 collective-permute-start.2
  197.5 64.7 %conditional.3 = (bf16[640,4096]{1,0:T(8,128)(2,1)}) conditional(s32[]{:T(128)} %bitcast.5, () %tuple.22, bf16[640,4096]{1,0:T(8,128)(2,1)} %get-tuple-element.22), branch_computations={%region_2.3_spmd, %region_3.4_spmd} | conditional | bytes 10485768 | solution.py:363
  197.5 64.7 %all_to_all.19 = bf16[16,40,4096]{2,1,0:T(8,128)(2,1)} all-to-all(bf16[16,40,4096]{2,1,0:T(8,128)(2,1)} %bitcast.33), channel_id=1, replica_groups=mesh['dp'=8,'expert'=16] {'expert'}, dimensions={0} | all-to-all | bytes 10485760 | tf_op jit(solution)/shard_map/cond/branch_1_fun/all_to_all | solution.py:365
  262.2 0.0 collective-permute-done
  262.2 0.0 copy-start
  262.2 0.0 collective-permute-done.1
  262.3 0.0 collective-permute-done.2
  262.3 1.1 copy-done
  263.3 2.3 add_add_fusion
  265.6 0.1 dynamic-slice_bitcast_fusion.4
  265.7 0.1 collective-permute-start.3
  265.8 8.0 %combine.1 = bf16[256,4096]{1,0:T(8,128)(2,1)} custom-call(s32[2,256]{1,0:T(2,128)} %bitcast.42, bf16[640,4096]{1,0:T(8,128)(2,1)} %get-tuple-element.34.ret_ref), custom_call_target="tpu_custom_call" | custom-call | flops 1342177280 | bytes 7340032 | tf_op jit(solution)/shard_map/combine/pallas_call | solution.py:160
  273.7 0.0 collective-permute-done.3
  273.8 0.1 bitcast_add_fusion
  273.8 0.8 slice.12
  274.6 0.6 slice.13
Async XLA Ops:
  7.2 143.1 %all-gather.2.cloned.1.call-start = ((), (), s32[]{:S(2)}) async-start(), calls=%async_computation.2 | async-start | bytes 2801664 | tf_op jit(solution)/shard_map/all_gather | solution.py:395
  191.9 70.3 %collective-permute-start = (f32[64,4864]{1,0:T(8,128)}, f32[64,4864]{1,0:T(8,128)S(1)}, u32[]{:S(2)}, u32[]{:S(2)}) collective-permute-start(f32[64,4864]{1,0:T(8,128)} %get-tuple-element.31), channel_id=1, source_target_pairs={{0,32},{16,48},{32,64},{48,80},{64,96},{80,112},{96,0},{112,16},{1... | collective-permute-start | bytes 3735560 | tf_op jit(solution)/shard_map/ppermute | solution.py:355
  193.4 68.9 %collective-permute-start.1 = (f32[64,4864]{1,0:T(8,128)}, f32[64,4864]{1,0:T(8,128)}, u32[]{:S(2)}, u32[]{:S(2)}) collective-permute-start(f32[64,4864]{1,0:T(8,128)} %get-tuple-element.30), channel_id=1, source_target_pairs={{0,64},{16,80},{32,96},{48,112},{64,0},{80,16},{96,32},{112,48},{1... | collective-permute-start | bytes 3735560 | tf_op jit(solution)/shard_map/ppermute | solution.py:355
  196.1 66.1 %collective-permute-start.2 = (f32[64,4864]{1,0:T(8,128)}, f32[64,4864]{1,0:T(8,128)}, u32[]{:S(2)}, u32[]{:S(2)}) collective-permute-start(f32[64,4864]{1,0:T(8,128)} %get-tuple-element.29), channel_id=1, source_target_pairs={{0,96},{16,112},{32,0},{48,16},{64,32},{80,48},{96,64},{112,80},{1... | collective-permute-start | bytes 3735560 | tf_op jit(solution)/shard_map/ppermute | solution.py:355
  262.2 1.1 copy-start
  265.7 8.1 %collective-permute-start.3 = (f32[32,4864]{1,0:T(8,128)S(1)}, f32[32,4864]{1,0:T(8,128)S(1)}, u32[]{:S(2)}, u32[]{:S(2)}) collective-permute-start(f32[32,4864]{1,0:T(8,128)S(1)} %dynamic-slice_bitcast_fusion.4), channel_id=1, source_target_pairs={{0,16},{16,0},{32,48},{48,32},{64,80},{80,64},{96,112},{112,96},{1... | collective-permute-start | bytes 1867784 | tf_op jit(solution)/shard_map/ppermute | solution.py:415
Sparse Core Ops, SparseCore 0:
  10.3 28.2 all-gather.1

commit v2 on v1

--- a/solution.py
+++ b/solution.py
@@ -22,7 +22,7 @@
     return jnp.dot(left_side, right_side, preferred_element_type=jnp.float32)
 
 
-def slot_masks(idx, experts, capacity):
+def route_slots(idx, experts, capacity):
     routes, tok_rows = idx.shape
     names = lax.broadcasted_iota(jnp.int32, (experts, tok_rows), 0)
     members = [(idx[k : k + 1, :] == names).astype(jnp.float32) for k in range(routes)]
@@ -31,12 +31,11 @@
         < lax.broadcasted_iota(jnp.int32, (tok_rows, tok_rows), 1)
     ).astype(jnp.bfloat16)
     running = matmul(sum(members).astype(jnp.bfloat16), before)
-    rows = lax.broadcasted_iota(jnp.int32, (experts * capacity, tok_rows), 0)
-    masks = []
-    for k, member in enumerate(members):
-        position = jnp.sum(running * member, axis=0, keepdims=True).astype(jnp.int32)
-        masks.append(rows == idx[k : k + 1, :] * capacity + position)
-    return masks
+    return [
+        idx[k : k + 1, :] * capacity
+        + jnp.sum(running * member, axis=0, keepdims=True).astype(jnp.int32)
+        for k, member in enumerate(members)
+    ]
 
 
 def dispatch_kernel(
@@ -79,7 +78,8 @@
 
     @pl.when(step == 0)
     def _():
-        masks = slot_masks(idx_ref[...], experts, capacity)
+        rows = lax.broadcasted_iota(jnp.int32, select.shape, 0)
+        masks = [rows == slots for slots in route_slots(idx_ref[...], experts, capacity)]
         filled = sum(m.astype(jnp.float32) for m in masks)
         weight[...] = sum(
             jnp.sum(jnp.where(m, prob_ref[k : k + 1, :], 0.0), axis=1, keepdims=True)
@@ -147,15 +147,21 @@
 def combine_kernel(experts, capacity, idx_ref, ret_ref, out_ref, select):
     @pl.when(pl.program_id(0) == 0)
     def _():
-        filled = sum(m.astype(jnp.float32) for m in slot_masks(idx_ref[...], experts, capacity))
-        select[...] = filled.T.astype(jnp.bfloat16)
+        slots = route_slots(idx_ref[...], experts, capacity)
+        rows = lax.broadcasted_iota(jnp.int32, (8, slots[0].shape[1]), 0)
+        table = sum(jnp.where(rows == k, s.astype(jnp.float32), 0.0) for k, s in enumerate(slots))
+        table = table.T.astype(jnp.int32)
+        lanes = lax.broadcasted_iota(jnp.int32, select.shape, 1)
+        select[...] = sum(
+            (lanes == table[:, k : k + 1]).astype(jnp.float32) for k in range(len(slots))
+        ).astype(jnp.bfloat16)
 
     out_ref[...] = matmul(select[...], ret_ref[...]).astype(jnp.bfloat16)
 
 
 def combine(idx, returned, experts, capacity):
     tok_rows, width = idx.shape[1], returned.shape[1]
-    block = 512
+    block = 1024
     rows = returned.shape[0]
     return pl.pallas_call(
         functools.partial(combine_kernel, experts, capacity),
@@ -179,13 +185,26 @@
 
 def expert_kernel(
     rank,
+    chips,
     got_ref,
-    held_ref,
     gate_ref,
     up_ref,
     down_ref,
+    *refs,
+):
+    held_refs, route_out, part_outs = refs[:chips], refs[chips], refs[chips + 1 : 2 * chips + 1]
+    expert_body(rank, got_ref, gate_ref, up_ref, down_ref, held_refs, route_out, part_outs, *refs[2 * chips + 1 :])
+
+
+def expert_body(
+    rank,
+    got_ref,
+    gate_ref,
+    up_ref,
+    down_ref,
+    held_refs,
     route_out,
-    part_out,
+    part_outs,
     feat,
     cot,
     tenant,
@@ -204,7 +223,7 @@
 ):
     width = feat.shape[1]
     hidden = down.shape[0]
-    groups = held_ref.shape[0]
+    groups, chip_rows = low_held.shape[0], held_refs[0].shape[0]
     block = 256
     step = 512
     parts = hidden // block
@@ -213,9 +232,18 @@
         (
             (got_ref.at[:, pl.ds(2 * width, LANES)], tenant),
             (got_ref.at[:, pl.ds(0, width)], feat),
-            (held_ref.at[:, pl.ds(0, width)], low_held),
-        ),
-        ((gate_ref, gate), (held_ref.at[:, pl.ds(width, hidden)], high_held)),
+            *(
+                (held.at[:, pl.ds(0, width)], low_held.at[pl.ds(c * chip_rows, chip_rows)])
+                for c, held in enumerate(held_refs)
+            ),
+        ),
+        (
+            (gate_ref, gate),
+            *(
+                (held.at[:, pl.ds(width, hidden)], high_held.at[pl.ds(c * chip_rows, chip_rows)])
+                for c, held in enumerate(held_refs)
+            ),
+        ),
         ((up_ref, up),),
         ((got_ref.at[:, pl.ds(width, width)], cot), (down_ref, down)),
     )
@@ -276,17 +304,19 @@
     up_sum[...] = adapter_scale * jnp.where(
         is_gate, matmul(low_t, grads[:, :hidden]), matmul(low_t, grads[:, hidden:])
     )
-    leaving = [
-        pltpu.make_async_copy(up_sum, part_out.at[:, pl.ds(width, hidden)], out_sems.at[0])
-    ]
-    leaving[-1].start()
+    leaving = []
+
+    def leave(source, target):
+        leaving.append(pltpu.make_async_copy(source, target, out_sems.at[len(leaving)]))
+        leaving[-1].start()
+
+    for c, part_out in enumerate(part_outs):
+        leave(up_sum.at[pl.ds(c * chip_rows, chip_rows)], part_out.at[:, pl.ds(width, hidden)])
     for i in range(width // step):
         at = pl.ds(i * step, step)
         down_sum[:, at] = adapter_scale * matmul(back_t, feat[:, at])
-        leaving.append(
-            pltpu.make_async_copy(down_sum.at[:, at], part_out.at[:, at], out_sems.at[len(leaving)])
-        )
-        leaving[-1].start()
+    for c, part_out in enumerate(part_outs):
+        leave(down_sum.at[pl.ds(c * chip_rows, chip_rows)], part_out.at[:, pl.ds(0, width)])
     for i in range(width // step):
         at = pl.ds(i * step, step)
         cot[:, at] = (
@@ -294,27 +324,25 @@
             + contract_last(grads[:, hidden:], up[at])
             + adapter_scale * matmul(low_back, low_held[:, at])
         ).astype(jnp.bfloat16)
-        leaving.append(
-            pltpu.make_async_copy(cot.at[:, at], route_out.at[:, at], out_sems.at[len(leaving)])
-        )
-        leaving[-1].start()
+        leave(cot.at[:, at], route_out.at[:, at])
     for copy in leaving:
         copy.wait()
 
 
-def expert_pass(received, held, gate_matrix, up_matrix, down_weight, rank):
+def expert_pass(received, gate_matrix, up_matrix, down_weight, held, rank):
     rows = received.shape[0]
     width, hidden = gate_matrix.shape
-    groups = held.shape[0]
+    chips, chip_rows = len(held), held[0].shape[0]
+    groups = chips * chip_rows
     anywhere = pl.BlockSpec(memory_space=pl.ANY)
     return pl.pallas_call(
-        functools.partial(expert_kernel, rank),
+        functools.partial(expert_kernel, rank, chips),
         out_shape=(
             jax.ShapeDtypeStruct((rows, width), jnp.bfloat16),
-            jax.ShapeDtypeStruct((groups, width + hidden), jnp.float32),
-        ),
-        in_specs=[anywhere] * 5,
-        out_specs=(anywhere, anywhere),
+            *[jax.ShapeDtypeStruct((chip_rows, width + hidden), jnp.float32)] * chips,
+        ),
+        in_specs=[anywhere] * (4 + chips),
+        out_specs=(anywhere,) * (1 + chips),
         scratch_shapes=[
             pltpu.VMEM((rows, width), jnp.bfloat16),
             pltpu.VMEM((rows, width), jnp.bfloat16),
@@ -329,8 +357,8 @@
             pltpu.VMEM((groups, hidden), jnp.float32),
             pltpu.VMEM((rows, hidden), jnp.float32),
             pltpu.VMEM((rows, hidden), jnp.float32),
-            pltpu.SemaphoreType.DMA((8,)),
-            pltpu.SemaphoreType.DMA((1 + 2 * (width // 512),)),
+            pltpu.SemaphoreType.DMA((6 + 2 * chips,)),
+            pltpu.SemaphoreType.DMA((2 * chips + width // 512,)),
         ],
         compiler_params=pltpu.CompilerParams(vmem_limit_bytes=VMEM_BYTES),
         cost_estimate=pl.CostEstimate(
@@ -339,24 +367,16 @@
             transcendentals=rows * hidden,
         ),
         name="expert_pass",
-    )(received, held, gate_matrix, up_matrix, down_weight)
-
-
-def chip_sums(part):
-    chips = part.shape[0]
+    )(received, gate_matrix, up_matrix, down_weight, *held)
+
+
+def along_x(rows, step):
     devices = lax.axis_size("dp")
-    per_chip = devices // chips
-    chip = lax.axis_index("dp") // per_chip
-    own = lax.dynamic_index_in_dim(part, chip, 0, keepdims=False)
-    arrived = []
-    for step in range(1, chips):
-        sent = lax.dynamic_index_in_dim(part, (chip + step) % chips, 0, keepdims=False)
-        arrived.append(
-            lax.ppermute(
-                sent, "dp", [(i, (i + per_chip * step) % devices) for i in range(devices)]
-            )
-        )
-    return own, arrived
+    return lax.ppermute(rows, "dp", [(i, (i + 2 * step) % devices) for i in range(devices)])
+
+
+def other_core(rows):
+    return lax.ppermute(rows, "dp", [(i, i ^ 1) for i in range(lax.axis_size("dp"))])
 
 
 def exchange(named, rows):
@@ -386,35 +406,35 @@
     routes = routed_expert_index.shape[1]
     hidden = frozen_gate_weight.shape[2]
     rank = adapter_down_matrices.shape[3]
-    groups = tenants * rank
     capacity = 5 * tok_rows * routes // (4 * experts)
     idx = routed_expert_index.T
     prob = router_gate_weights.T
-    tenant = token_tenant_index.reshape(1, tok_rows)
+    me = lax.axis_index("dp")
+    chips = tenants // 2
+    tenant = (me // 2 - token_tenant_index // 2) % chips * 2 + (me + token_tenant_index) % 2
+    tenant = tenant.reshape(1, tok_rows)
     adapters = jnp.concatenate([adapter_down_matrices[0, 0], adapter_up_matrices[0, 0]], axis=-1)
-    held = lax.all_gather(adapters, "dp", axis=0, tiled=True)
+    adapters = adapters.reshape(2 * rank, width + hidden)
+    pair = jnp.concatenate([adapters, other_core(adapters)], axis=0)
+    held = [pair] + [along_x(pair, step) for step in range(1, chips)]
+    named = me < tenants
     sent = dispatch(idx, prob, tenant, tokens, cotangent, experts, capacity)
-    named = routed_expert_index[0, 0] >= 0
     received = exchange(named, sent)
-    received, held = lax.optimization_barrier((received, held))
-    route_grad, part = expert_pass(
+    received, *held = lax.optimization_barrier((received, *held))
+    route_grad, own, *parts = expert_pass(
         received,
-        held.reshape(2 * groups, width + hidden),
         frozen_gate_weight[0],
         frozen_up_weight[0],
         frozen_down_weight[0],
+        held,
         rank,
     )
-    own, arrived = chip_sums(part.reshape(tenants // 2, 4 * rank, width + hidden))
+    arrived = [along_x(part, -step) for step, part in enumerate(parts, 1)]
     returned = exchange(named, route_grad)
     returned, own, *arrived = lax.optimization_barrier((returned, own, *arrived))
     token_grads = combine(idx, returned, experts, capacity)
-    total = sum(arrived, own).reshape(2, 2 * rank, width + hidden)
-    core = lax.axis_index("dp") % 2
-    theirs = lax.dynamic_index_in_dim(total, 1 - core, 0, keepdims=False)
-    owned = lax.dynamic_index_in_dim(total, core, 0, keepdims=False) + lax.ppermute(
-        theirs, "dp", [(i, i ^ 1) for i in range(tenants)]
-    )
+    total = sum(arrived, own)
+    owned = total[: 2 * rank] + other_core(total[2 * rank :])
     down_owned = owned[:, :width].reshape(1, 1, 2, rank, width)
     up_owned = owned[:, width:].reshape(1, 1, 2, rank, hidden)
     return token_grads, down_owned, up_owned

time: 284 us -> 267 us (0.940)
  between operations: 14.8 us -> 0.76 us
  local copies, waits for them, and re-layouts: 8.2 us -> 2.78 us
  starting transfers between devices: 5.77 us -> 8.71 us
    squeeze x2 -> x0, local copies, waits for them, and re-layouts: 4.46 us -> none  [the longest x1 4.41 us: chip_sums(): lax.dynamic_index_in_dim(part, (chip + step) % chips, 0, keepdims=False)]
    ppermute x4 -> x8, starting transfers between devices: 5.73 us -> 8.71 us  [the longest x6 8.54 us: along_x(): lax.ppermute(rows, 'dp', [(i, (i + 2 * step) % devices) for i in range(de...]
  transfers between devices with their start and end apart: 5 -> 8, of which waited for: 0 -> 1; matrix products, arithmetic and copies ran while one was open for 0% -> 0% of each run, Pallas kernels for 6% -> 6%
where the time goes in v2:
time: 267 us; the launch traced here: 265 us
  blocking collectives  193 us (72%)
  Pallas kernels  52.8 us (20%)
  starting transfers between devices  8.71 us (3%)
  other arithmetic  4.57 us (2%)
  local copies, waits for them, and re-layouts  2.78 us (1%)
    all_to_all x2, blocking collectives, exchange(): lax.all_to_all(r, 'expert', split_axis=0, concat_axis=0, tiled=True)  193 us
    pallas_call x1, Pallas kernels, expert_pass(): pl.pallas_call(functools.partial(expert_kernel, rank, chips), out_shape=(...  37.2 us
    pallas_call x1, Pallas kernels, dispatch(): pl.pallas_call(functools.partial(dispatch_kernel, experts, capacity), out...  9.66 us
    ppermute x6, starting transfers between devices, along_x(): lax.ppermute(rows, 'dp', [(i, (i + 2 * step) % devices) for i in range(de...  8.54 us
    pallas_call x1, Pallas kernels, combine(): pl.pallas_call(functools.partial(combine_kernel, experts, capacity), out_...  5.97 us
  transfers between devices with their start and end apart: 8, of which 1 were waited for; matrix products, arithmetic and copies ran while one was open for 0% of the time, Pallas kernels for 6%

profile of v2, /device:TPU:0, one launch (start us, length us, event | category | flops | bytes accessed | tf_op | source)
XLA Modules:
  0.0 264.6 jit_solution(17866126301602774144)
XLA Ops:
  0.6 0.0 copy-start.2
  0.6 1.0 pad_maximum_fusion.1
  1.6 0.1 collective-permute-start
  1.7 1.6 collective-permute-done
  3.3 1.0 pad_maximum_fusion.refs_0_
  4.4 0.0 copy-start.1
  4.4 1.6 collective-permute-start.1
  6.0 2.7 %collective-permute-start.2 = (bf16[64,4864]{1,0:T(8,128)(2,1)S(1)}, bf16[64,4864]{1,0:T(8,128)(2,1)S(1)}, u32[]{:S(2)}, u32[]{:S(2)}) collective-permute-start(bf16[64,4864]{1,0:T(8,128)(2,1)S(1)} %pad_maximum_fusion.refs_0_), channel_id=1, source_target_pairs={{0,64},{16,80},{32,96},{48,112},{64,0},{80,16},{96,32},{112,48},{1... | collective-permute-start | bytes 1867784 | tf_op jit(solution)/shard_map/ppermute | solution.py:375
  8.7 1.4 collective-permute-start.3
  10.2 0.0 copy-done.2
  10.2 0.6 fusion
  10.8 9.7 %dispatch.1 = bf16[640,8320]{1,0:T(8,128)(2,1)} custom-call(s32[2,256]{1,0:T(2,128)} %bitcast.24, f32[2,256]{1,0:T(2,128)} %bitcast.27, s32[1,256]{1,0:T(1,128)} %bitcast.26, bf16[256,4096]{1,0:T(8,128)(2,1)} %tok_ref.1, bf16[256,4096]{1,0:T(8,128)(2,1)} %cot_ref.1), custom_call_target="tpu_custom_call" | custom-call | flops 2684354560 | bytes 14680064 | tf_op jit(solution)/shard_map/dispatch/pallas_call | solution.py:116
  20.4 0.0 copy-done.1
  20.4 127.4 %conditional.2 = (bf16[640,8320]{1,0:T(8,128)(2,1)}) conditional(s32[]{:T(128)} %convert_element_type.4, () %tuple.23, bf16[640,8320]{1,0:T(8,128)(2,1)} %dispatch.1), branch_computations={%region_0.1_spmd, %region_1.2_spmd} | conditional | bytes 21299208 | solution.py:383
  20.4 127.4 %all_to_all.18 = bf16[16,40,8320]{2,1,0:T(8,128)(2,1)} all-to-all(bf16[16,40,8320]{2,1,0:T(8,128)(2,1)} %bitcast.14), channel_id=1, replica_groups=mesh['dp'=8,'expert'=16] {'expert'}, dimensions={0} | all-to-all | bytes 21299200 | tf_op jit(solution)/shard_map/cond/branch_1_fun/all_to_all | solution.py:385
  147.9 0.0 collective-permute-done.1.refs_1_
  147.9 0.0 copy-start.3
  147.9 0.0 collective-permute-done.2.refs_2_
  147.9 0.0 copy-start.4
  147.9 0.0 collective-permute-done.3.refs_3_
  147.9 0.0 copy-start.5
  147.9 0.8 copy-done.3
  148.7 0.2 copy-done.4
  148.9 0.2 copy-done.5
  149.2 37.2 %expert_pass.1 = (bf16[640,4096]{1,0:T(8,128)(2,1)}, f32[64,4864]{1,0:T(8,128)}, f32[64,4864]{1,0:T(8,128)}, f32[64,4864]{1,0:T(8,128)}, f32[64,4864]{1,0:T(8,128)}) custom-call(bf16[640,8320]{1,0:T(8,128)(2,1)} %get-tuple-element.41.got_ref, bf16[4096,768]{1,0:T(8,128)(2,1)} %bitcast.28, bf16[4096,768]{1,0:T(8,128)(2,1)} %bitcast.29, ...), custom_call_target="tpu_custom_call" | custom-call | flops 24159191040 | bytes 34603008 | tf_op jit(solution)/shard_map/expert_pass/pallas_call | solution.py:338
  186.4 0.4 collective-permute-start.4
  186.7 2.4 collective-permute-start.5
  189.1 0.0 collective-permute-start.6
  189.1 0.0 copy-start
  189.1 65.9 %conditional.3 = (bf16[640,4096]{1,0:T(8,128)(2,1)}) conditional(s32[]{:T(128)} %convert_element_type.4, () %tuple.22, bf16[640,4096]{1,0:T(8,128)(2,1)} %get-tuple-element.31), branch_computations={%region_2.3_spmd, %region_3.4_spmd} | conditional | bytes 10485768 | solution.py:383
  189.1 65.9 %all_to_all.19 = bf16[16,40,4096]{2,1,0:T(8,128)(2,1)} all-to-all(bf16[16,40,4096]{2,1,0:T(8,128)(2,1)} %bitcast.17), channel_id=1, replica_groups=mesh['dp'=8,'expert'=16] {'expert'}, dimensions={0} | all-to-all | bytes 10485760 | tf_op jit(solution)/shard_map/cond/branch_1_fun/all_to_all | solution.py:385
  255.0 0.0 collective-permute-done.4
  255.0 0.0 collective-permute-done.5
  255.0 0.0 collective-permute-done.6
  255.0 0.0 copy-done
  255.0 1.9 add_add_fusion
  257.0 0.1 collective-permute-start.7
  257.1 6.0 %combine.1 = bf16[256,4096]{1,0:T(8,128)(2,1)} custom-call(s32[2,256]{1,0:T(2,128)} %bitcast.25, bf16[640,4096]{1,0:T(8,128)(2,1)} %get-tuple-element.42.ret_ref), custom_call_target="tpu_custom_call" | custom-call | flops 1342177280 | bytes 7340032 | tf_op jit(solution)/shard_map/combine/pallas_call | solution.py:166
  263.0 0.0 collective-permute-done.7
  263.0 0.1 slice_add_fusion
  263.1 0.8 slice.18
  263.9 0.6 slice.19
  (1 shorter events, 0.0 us)
Async XLA Ops:
  0.6 9.6 %copy-start.2 = (s32[256]{0:T(256)S(1)}, s32[256]{0:T(256)}, u32[]{:S(2)}) copy-start(s32[256]{0:T(256)} %param.18) | copy-start | bytes 3076
  1.6 1.7 collective-permute-start
  4.4 16.1 %copy-start.1 = (bf16[64,4864]{1,0:T(8,128)(2,1)}, bf16[64,4864]{1,0:T(8,128)(2,1)S(1)}, u32[]{:S(2)}) copy-start(bf16[64,4864]{1,0:T(8,128)(2,1)S(1)} %pad_maximum_fusion.refs_0_) | copy-start | bytes 1867780
  4.4 143.5 %collective-permute-start.1 = (bf16[64,4864]{1,0:T(8,128)(2,1)S(1)}, bf16[64,4864]{1,0:T(8,128)(2,1)S(1)}, u32[]{:S(2)}, u32[]{:S(2)}) collective-permute-start(bf16[64,4864]{1,0:T(8,128)(2,1)S(1)} %pad_maximum_fusion.refs_0_), channel_id=1, source_target_pairs={{0,32},{16,48},{32,64},{48,80},{64,96},{80,112},{96,0},{112,16},{1... | collective-permute-start | bytes 1867784 | tf_op jit(solution)/shard_map/ppermute | solution.py:375
  6.0 141.9 %collective-permute-start.2 = (bf16[64,4864]{1,0:T(8,128)(2,1)S(1)}, bf16[64,4864]{1,0:T(8,128)(2,1)S(1)}, u32[]{:S(2)}, u32[]{:S(2)}) collective-permute-start(bf16[64,4864]{1,0:T(8,128)(2,1)S(1)} %pad_maximum_fusion.refs_0_), channel_id=1, source_target_pairs={{0,64},{16,80},{32,96},{48,112},{64,0},{80,16},{96,32},{112,48},{1... | collective-permute-start | bytes 1867784 | tf_op jit(solution)/shard_map/ppermute | solution.py:375
  8.7 139.1 %collective-permute-start.3 = (bf16[64,4864]{1,0:T(8,128)(2,1)S(1)}, bf16[64,4864]{1,0:T(8,128)(2,1)S(1)}, u32[]{:S(2)}, u32[]{:S(2)}) collective-permute-start(bf16[64,4864]{1,0:T(8,128)(2,1)S(1)} %pad_maximum_fusion.refs_0_), channel_id=1, source_target_pairs={{0,96},{16,112},{32,0},{48,16},{64,32},{80,48},{96,64},{112,80},{1... | collective-permute-start | bytes 1867784 | tf_op jit(solution)/shard_map/ppermute | solution.py:375
  147.9 0.9 copy-start.3
  147.9 1.1 copy-start.4
  147.9 1.3 copy-start.5
  186.4 68.6 %collective-permute-start.4 = (f32[64,4864]{1,0:T(8,128)}, f32[64,4864]{1,0:T(8,128)S(1)}, u32[]{:S(2)}, u32[]{:S(2)}) collective-permute-start(f32[64,4864]{1,0:T(8,128)} %get-tuple-element.33), channel_id=1, source_target_pairs={{0,96},{16,112},{32,0},{48,16},{64,32},{80,48},{96,64},{112,80},{1... | collective-permute-start | bytes 3735560 | tf_op jit(solution)/shard_map/ppermute | solution.py:375
  186.7 68.3 %collective-permute-start.5 = (f32[64,4864]{1,0:T(8,128)}, f32[64,4864]{1,0:T(8,128)}, u32[]{:S(2)}, u32[]{:S(2)}) collective-permute-start(f32[64,4864]{1,0:T(8,128)} %get-tuple-element.34), channel_id=1, source_target_pairs={{0,64},{16,80},{32,96},{48,112},{64,0},{80,16},{96,32},{112,48},{1... | collective-permute-start | bytes 3735560 | tf_op jit(solution)/shard_map/ppermute | solution.py:375
  189.1 65.9 %collective-permute-start.6 = (f32[64,4864]{1,0:T(8,128)}, f32[64,4864]{1,0:T(8,128)}, u32[]{:S(2)}, u32[]{:S(2)}) collective-permute-start(f32[64,4864]{1,0:T(8,128)} %get-tuple-element.35), channel_id=1, source_target_pairs={{0,32},{16,48},{32,64},{48,80},{64,96},{80,112},{96,0},{112,16},{1... | collective-permute-start | bytes 3735560 | tf_op jit(solution)/shard_map/ppermute | solution.py:375
  189.1 65.9 %copy-start = (f32[64,4864]{1,0:T(8,128)S(1)}, f32[64,4864]{1,0:T(8,128)}, u32[]{:S(2)}) copy-start(f32[64,4864]{1,0:T(8,128)} %get-tuple-element.37) | copy-start | bytes 3735556
  257.0 6.1 %collective-permute-start.7 = (f32[32,4864]{1,0:T(8,128)S(1)}, f32[32,4864]{1,0:T(8,128)S(1)}, u32[]{:S(2)}, u32[]{:S(2)}) collective-permute-start(f32[32,4864]{1,0:T(8,128)S(1)} %slice.17), channel_id=1, source_target_pairs={{0,16},{16,0},{32,48},{48,32},{64,80},{80,64},{96,112},{112,96},{1... | collective-permute-start | bytes 1867784 | tf_op jit(solution)/shard_map/ppermute | solution.py:379

commit v3 on v2

--- a/solution.py
+++ b/solution.py
@@ -112,7 +112,7 @@
 def dispatch(idx, prob, tenant, tokens, cotangent, experts, capacity):
     tok_rows, width = tokens.shape
     rows = experts * capacity
-    block = 512
+    block = 2048
     return pl.pallas_call(
         functools.partial(dispatch_kernel, experts, capacity),
         out_shape=jax.ShapeDtypeStruct((rows, 2 * width + LANES), jnp.bfloat16),
@@ -161,7 +161,7 @@
 
 def combine(idx, returned, experts, capacity):
     tok_rows, width = idx.shape[1], returned.shape[1]
-    block = 1024
+    block = 2048
     rows = returned.shape[0]
     return pl.pallas_call(
         functools.partial(combine_kernel, experts, capacity),
@@ -218,115 +218,144 @@
     up_sum,
     gate_pre,
     up_pre,
+    low,
+    low_t,
+    back_t,
+    high_gate,
+    high_up,
+    first_sems,
     sems,
     out_sems,
+    route_sems,
 ):
     width = feat.shape[1]
     hidden = down.shape[0]
     groups, chip_rows = low_held.shape[0], held_refs[0].shape[0]
     block = 256
-    step = 512
+    step = 1024
     parts = hidden // block
 
-    stages = (
-        (
-            (got_ref.at[:, pl.ds(2 * width, LANES)], tenant),
-            (got_ref.at[:, pl.ds(0, width)], feat),
-            *(
-                (held.at[:, pl.ds(0, width)], low_held.at[pl.ds(c * chip_rows, chip_rows)])
-                for c, held in enumerate(held_refs)
-            ),
-        ),
-        (
-            (gate_ref, gate),
-            *(
-                (held.at[:, pl.ds(width, hidden)], high_held.at[pl.ds(c * chip_rows, chip_rows)])
-                for c, held in enumerate(held_refs)
-            ),
-        ),
-        ((up_ref, up),),
-        ((got_ref.at[:, pl.ds(width, width)], cot), (down_ref, down)),
-    )
-    copies = []
-    for stage in stages:
-        first = sum(len(c) for c in copies)
-        copies.append(
-            [
-                pltpu.make_async_copy(source, target, sems.at[first + i])
-                for i, (source, target) in enumerate(stage)
-            ]
+    quarter = width // 4
+
+    def first_copies(q):
+        at = pl.ds(pl.multiple_of(q * quarter, quarter), quarter)
+        return (
+            pltpu.make_async_copy(got_ref.at[:, at], feat.at[:, at], first_sems.at[0, q]),
+            pltpu.make_async_copy(gate_ref.at[at], gate.at[at], first_sems.at[1, q]),
         )
-    ahead = 2
-    for stage in copies[:ahead]:
-        for copy in stage:
+
+    later = [[], [], []]
+
+    def plan(stage, source, target):
+        number = sum(len(c) for c in later)
+        later[stage].append(pltpu.make_async_copy(source, target, sems.at[number]))
+
+    plan(0, got_ref.at[:, pl.ds(2 * width, LANES)], tenant)
+    for c, held in enumerate(held_refs):
+        rows = pl.ds(c * chip_rows, chip_rows)
+        plan(0, held.at[:, pl.ds(0, width)], low_held.at[rows])
+        plan(0, held.at[:, pl.ds(width, hidden)], high_held.at[rows])
+    plan(1, up_ref, up)
+    plan(2, got_ref.at[:, pl.ds(width, width)], cot)
+    plan(2, down_ref, down)
+
+    def begin(copies):
+        for copy in copies:
             copy.start()
 
-    def arrive(i):
-        for copy in copies[i]:
+    def arrive(copies):
+        for copy in copies:
             copy.wait()
-        if i + ahead < len(copies):
-            for copy in copies[i + ahead]:
-                copy.start()
-
-    arrive(0)
+
+    begin(first_copies(0))
+    begin(first_copies(1))
+    gate_pre[...] = jnp.zeros_like(gate_pre)
+
+    def gate_step(q, carry):
+        arrive(first_copies(q))
+        pl.when(q < 2)(lambda: begin(first_copies(q + 2)))
+        pl.when(q == 2)(lambda: begin(later[0]))
+        pl.when(q == 3)(lambda: begin(later[1]))
+        at = pl.ds(pl.multiple_of(q * quarter, quarter), quarter)
+        for h in range(parts):
+            to = slice(h * block, (h + 1) * block)
+            gate_pre[:, to] += matmul(feat[:, at], gate[at, to])
+        return carry
+
+    lax.fori_loop(0, 4, gate_step, 0)
+    arrive(later[0])
+    begin(later[2])
     owner = lax.broadcasted_iota(jnp.int32, (1, groups), 1) // (2 * rank)
     selector = (tenant[:, 0:1].astype(jnp.int32) == owner).astype(jnp.float32)
-    low = (contract_last(feat[...], low_held[...]) * selector).astype(jnp.bfloat16)
-    arrive(1)
+    low[...] = (contract_last(feat[...], low_held[...]) * selector).astype(jnp.bfloat16)
     is_gate = lax.broadcasted_iota(jnp.int32, (groups, 1), 0) // rank % 2 == 0
     high = high_held[...].astype(jnp.float32)
-    high_gate = jnp.where(is_gate, high, 0.0).astype(jnp.bfloat16)
-    high_up = jnp.where(is_gate, 0.0, high).astype(jnp.bfloat16)
-    for h in range(parts):
-        at = slice(h * block, (h + 1) * block)
-        gate_pre[:, at] = matmul(feat[...], gate[:, at]) + adapter_scale * matmul(
-            low, high_gate[:, at]
+    high_gate[...] = jnp.where(is_gate, high, 0.0).astype(jnp.bfloat16)
+    high_up[...] = jnp.where(is_gate, 0.0, high).astype(jnp.bfloat16)
+    arrive(later[1])
+
+    def up_step(h, carry):
+        at = pl.ds(pl.multiple_of(h * block, block), block)
+        up_pre[:, at] = matmul(feat[...], up[:, at]) + adapter_scale * matmul(
+            low[...], high_up[:, at]
         )
-    arrive(2)
-    for h in range(parts):
-        at = slice(h * block, (h + 1) * block)
-        up_pre[:, at] = matmul(feat[...], up[:, at]) + adapter_scale * matmul(low, high_up[:, at])
-    arrive(3)
-    for h in range(parts):
-        at = slice(h * block, (h + 1) * block)
-        after = slice(hidden + h * block, hidden + (h + 1) * block)
+        return carry
+
+    lax.fori_loop(0, parts, up_step, 0)
+    arrive(later[2])
+
+    def back_step(h, carry):
+        at = pl.ds(pl.multiple_of(h * block, block), block)
+        after = pl.ds(pl.multiple_of(hidden + h * block, block), block)
         back = contract_last(cot[...], down[at])
-        pre = gate_pre[:, at]
+        pre = gate_pre[:, at] + adapter_scale * matmul(low[...], high_gate[:, at])
         sig = jax.nn.sigmoid(pre)
         grads[:, at] = (back * up_pre[:, at] * (sig + pre * sig * (1.0 - sig))).astype(jnp.bfloat16)
         grads[:, after] = (back * pre * sig).astype(jnp.bfloat16)
-    low_back = contract_last(grads[:, :hidden], high_gate) + contract_last(
-        grads[:, hidden:], high_up
+        return carry
+
+    lax.fori_loop(0, parts, back_step, 0)
+    low_back = contract_last(grads[:, :hidden], high_gate[...]) + contract_last(
+        grads[:, hidden:], high_up[...]
     )
     low_back = (low_back * selector).astype(jnp.bfloat16)
-    back_t = low_back.astype(jnp.float32).T.astype(jnp.bfloat16)
-    low_t = low.astype(jnp.float32).T.astype(jnp.bfloat16)
-    up_sum[...] = adapter_scale * jnp.where(
-        is_gate, matmul(low_t, grads[:, :hidden]), matmul(low_t, grads[:, hidden:])
-    )
-    leaving = []
-
-    def leave(source, target):
-        leaving.append(pltpu.make_async_copy(source, target, out_sems.at[len(leaving)]))
-        leaving[-1].start()
-
-    for c, part_out in enumerate(part_outs):
-        leave(up_sum.at[pl.ds(c * chip_rows, chip_rows)], part_out.at[:, pl.ds(width, hidden)])
+    back_t[...] = low_back.astype(jnp.float32).T.astype(jnp.bfloat16)
+    low_t[...] = low[...].astype(jnp.float32).T.astype(jnp.bfloat16)
+    low[...] = low_back
+
+    for h in range(parts):
+        at = pl.ds(h * block, block)
+        after = pl.ds(hidden + h * block, block)
+        up_sum[:, at] = adapter_scale * jnp.where(
+            is_gate, matmul(low_t[...], grads[:, at]), matmul(low_t[...], grads[:, after])
+        )
     for i in range(width // step):
         at = pl.ds(i * step, step)
-        down_sum[:, at] = adapter_scale * matmul(back_t, feat[:, at])
+        down_sum[:, at] = adapter_scale * matmul(back_t[...], feat[:, at])
+    leaving = []
     for c, part_out in enumerate(part_outs):
-        leave(down_sum.at[pl.ds(c * chip_rows, chip_rows)], part_out.at[:, pl.ds(0, width)])
+        rows = pl.ds(c * chip_rows, chip_rows)
+        for source, at in ((up_sum, pl.ds(width, hidden)), (down_sum, pl.ds(0, width))):
+            leaving.append(
+                pltpu.make_async_copy(source.at[rows], part_out.at[:, at], out_sems.at[len(leaving)])
+            )
+    begin(leaving)
+
+    def route_copy(i):
+        at = pl.ds(i * step, step)
+        return pltpu.make_async_copy(cot.at[:, at], route_out.at[:, at], route_sems.at[i])
+
     for i in range(width // step):
         at = pl.ds(i * step, step)
         cot[:, at] = (
             contract_last(grads[:, :hidden], gate[at])
             + contract_last(grads[:, hidden:], up[at])
-            + adapter_scale * matmul(low_back, low_held[:, at])
+            + adapter_scale * matmul(low[...], low_held[:, at])
         ).astype(jnp.bfloat16)
-        leave(cot.at[:, at], route_out.at[:, at])
-    for copy in leaving:
-        copy.wait()
+        route_copy(i).start()
+    arrive(leaving)
+    for i in range(width // step):
+        route_copy(i).wait()
 
 
 def expert_pass(received, gate_matrix, up_matrix, down_weight, held, rank):
@@ -357,8 +386,15 @@
             pltpu.VMEM((groups, hidden), jnp.float32),
             pltpu.VMEM((rows, hidden), jnp.float32),
             pltpu.VMEM((rows, hidden), jnp.float32),
-            pltpu.SemaphoreType.DMA((6 + 2 * chips,)),
-            pltpu.SemaphoreType.DMA((2 * chips + width // 512,)),
+            pltpu.VMEM((rows, groups), jnp.bfloat16),
+            pltpu.VMEM((groups, rows), jnp.bfloat16),
+            pltpu.VMEM((groups, rows), jnp.bfloat16),
+            pltpu.VMEM((groups, hidden), jnp.bfloat16),
+            pltpu.VMEM((groups, hidden), jnp.bfloat16),
+            pltpu.SemaphoreType.DMA((2, 4)),
+            pltpu.SemaphoreType.DMA((4 + 2 * chips,)),
+            pltpu.SemaphoreType.DMA((2 * chips,)),
+            pltpu.SemaphoreType.DMA((width // 1024,)),
         ],
         compiler_params=pltpu.CompilerParams(vmem_limit_bytes=VMEM_BYTES),
         cost_estimate=pl.CostEstimate(
@@ -415,10 +451,11 @@
     tenant = tenant.reshape(1, tok_rows)
     adapters = jnp.concatenate([adapter_down_matrices[0, 0], adapter_up_matrices[0, 0]], axis=-1)
     adapters = adapters.reshape(2 * rank, width + hidden)
-    pair = jnp.concatenate([adapters, other_core(adapters)], axis=0)
-    held = [pair] + [along_x(pair, step) for step in range(1, chips)]
     named = me < tenants
     sent = dispatch(idx, prob, tenant, tokens, cotangent, experts, capacity)
+    sent, others = lax.optimization_barrier((sent, other_core(adapters)))
+    pair = jnp.concatenate([adapters, others], axis=0)
+    held = [pair] + [along_x(pair, step) for step in range(1, chips)]
     received = exchange(named, sent)
     received, *held = lax.optimization_barrier((received, *held))
     route_grad, own, *parts = expert_pass(

time: 267 us -> 259 us (0.970)
  Pallas kernels: 52.8 us -> 46.5 us
    pallas_call x1, Pallas kernels: 37.2 us -> 33.8 us  [expert_pass(): pl.pallas_call(functools.partial(expert_kernel, rank, chips), out_shape=(...]
  transfers between devices with their start and end apart: 8 -> 8, of which waited for: 1 -> 0; matrix products, arithmetic and copies ran while one was open for 0% -> 0% of each run, Pallas kernels for 6% -> 5%
where the time goes in v3:
time: 259 us; the launch traced here: 257 us
  blocking collectives  193 us (75%)
  Pallas kernels  46.5 us (18%)
  starting transfers between devices  10 us (4%)
  other arithmetic  4.26 us (2%)
  local copies, waits for them, and re-layouts  2.8 us (1%)
    all_to_all x2, blocking collectives, exchange(): lax.all_to_all(r, 'expert', split_axis=0, concat_axis=0, tiled=True)  193 us
    pallas_call x1, Pallas kernels, expert_pass(): pl.pallas_call(functools.partial(expert_kernel, rank, chips), out_shape=(...  33.8 us
    ppermute x6, starting transfers between devices, along_x(): lax.ppermute(rows, 'dp', [(i, (i + 2 * step) % devices) for i in range(de...  9.86 us
    pallas_call x1, Pallas kernels, dispatch(): pl.pallas_call(functools.partial(dispatch_kernel, experts, capacity), out...  7.43 us
    pallas_call x1, Pallas kernels, combine(): pl.pallas_call(functools.partial(combine_kernel, experts, capacity), out_...  5.2 us
  transfers between devices with their start and end apart: 8, of which 0 were waited for; matrix products, arithmetic and copies ran while one was open for 0% of the time, Pallas kernels for 5%

profile of v3, /device:TPU:0, one launch (start us, length us, event | category | flops | bytes accessed | tf_op | source)
XLA Modules:
  0.0 257.0 jit_solution(9291917185106796991)
XLA Ops:
  0.6 1.0 pad_maximum_fusion.1
  1.6 0.1 collective-permute-start
  1.7 1.3 fusion
  3.0 0.0 copy-start.1
  3.0 0.0 copy-start.3
  3.0 7.4 %dispatch.1 = bf16[640,8320]{1,0:T(8,128)(2,1)} custom-call(s32[2,256]{1,0:T(2,128)} %bitcast.24, f32[2,256]{1,0:T(2,128)} %bitcast.27, s32[1,256]{1,0:T(1,128)} %bitcast.26, bf16[256,4096]{1,0:T(8,128)(2,1)} %tok_ref.1, bf16[256,4096]{1,0:T(8,128)(2,1)} %cot_ref.1), custom_call_target="tpu_custom_call" | custom-call | flops 2684354560 | bytes 14680064 | tf_op jit(solution)/shard_map/dispatch/pallas_call | solution.py:116
  10.4 0.0 collective-permute-done
  10.5 0.0 copy-done.1
  10.5 0.0 copy-done.3
  10.5 0.0 copy-start.2
  10.5 2.9 %collective-permute-start.3 = (bf16[64,4864]{1,0:T(8,128)(2,1)S(1)}, bf16[64,4864]{1,0:T(8,128)(2,1)S(1)}, u32[]{:S(2)}, u32[]{:S(2)}) collective-permute-start(bf16[64,4864]{1,0:T(8,128)(2,1)S(1)} %pad_maximum_fusion.refs_0_), channel_id=1, source_target_pairs={{0,96},{16,112},{32,0},{48,16},{64,32},{80,48},{96,64},{112,80},{1... | collective-permute-start | bytes 1867784 | tf_op jit(solution)/shard_map/ppermute | solution.py:411
  13.4 0.8 collective-permute-start.2
  14.2 0.9 collective-permute-start.1
  15.1 0.0 copy-done.2
  15.1 127.8 %conditional.2 = (bf16[640,8320]{1,0:T(8,128)(2,1)}) conditional(s32[]{:T(128)} %convert_element_type.4, () %tuple.24, bf16[640,8320]{1,0:T(8,128)(2,1)} %dispatch.1), branch_computations={%region_0.1_spmd, %region_1.2_spmd} | conditional | bytes 21299208 | solution.py:419
  15.1 127.8 %all_to_all.18 = bf16[16,40,8320]{2,1,0:T(8,128)(2,1)} all-to-all(bf16[16,40,8320]{2,1,0:T(8,128)(2,1)} %bitcast.14), channel_id=1, replica_groups=mesh['dp'=8,'expert'=16] {'expert'}, dimensions={0} | all-to-all | bytes 21299200 | tf_op jit(solution)/shard_map/cond/branch_1_fun/all_to_all | solution.py:421
  142.9 0.0 collective-permute-done.3.refs_3_
  142.9 0.0 copy-start.4
  142.9 0.0 collective-permute-done.2.refs_2_
  142.9 0.0 copy-start.5
  142.9 0.0 collective-permute-done.1.refs_1_
  142.9 0.0 copy-start.6
  142.9 0.8 copy-done.4
  143.7 0.2 copy-done.5
  144.0 0.2 copy-done.6
  144.2 33.8 %expert_pass.1 = (bf16[640,4096]{1,0:T(8,128)(2,1)}, f32[64,4864]{1,0:T(8,128)}, f32[64,4864]{1,0:T(8,128)}, f32[64,4864]{1,0:T(8,128)}, f32[64,4864]{1,0:T(8,128)}) custom-call(bf16[640,8320]{1,0:T(8,128)(2,1)} %get-tuple-element.45.got_ref, bf16[4096,768]{1,0:T(8,128)(2,1)} %bitcast.28, bf16[4096,768]{1,0:T(8,128)(2,1)} %bitcast.29, ...), custom_call_target="tpu_custom_call" | custom-call | flops 24159191040 | bytes 34603008 | tf_op jit(solution)/shard_map/expert_pass/pallas_call | solution.py:367
  178.0 2.4 collective-permute-start.4
  180.5 1.5 collective-permute-start.5
  182.0 1.3 collective-permute-start.6
  183.3 0.0 copy-start
  183.3 64.9 %conditional.3 = (bf16[640,4096]{1,0:T(8,128)(2,1)}) conditional(s32[]{:T(128)} %convert_element_type.4, () %tuple.23, bf16[640,4096]{1,0:T(8,128)(2,1)} %get-tuple-element.35), branch_computations={%region_2.3_spmd, %region_3.4_spmd} | conditional | bytes 10485768 | solution.py:419
  183.3 64.9 %all_to_all.19 = bf16[16,40,4096]{2,1,0:T(8,128)(2,1)} all-to-all(bf16[16,40,4096]{2,1,0:T(8,128)(2,1)} %bitcast.17), channel_id=1, replica_groups=mesh['dp'=8,'expert'=16] {'expert'}, dimensions={0} | all-to-all | bytes 10485760 | tf_op jit(solution)/shard_map/cond/branch_1_fun/all_to_all | solution.py:421
  248.2 0.0 collective-permute-done.4
  248.2 0.0 collective-permute-done.5
  248.2 0.0 collective-permute-done.6
  248.2 0.0 copy-done
  248.2 1.9 add_add_fusion
  250.2 0.1 collective-permute-start.7
  250.3 5.2 %combine.1 = bf16[256,4096]{1,0:T(8,128)(2,1)} custom-call(s32[2,256]{1,0:T(2,128)} %bitcast.25, bf16[640,4096]{1,0:T(8,128)(2,1)} %get-tuple-element.46.ret_ref), custom_call_target="tpu_custom_call" | custom-call | flops 1342177280 | bytes 7340032 | tf_op jit(solution)/shard_map/combine/pallas_call | solution.py:166
  255.5 0.0 collective-permute-done.7
  255.5 0.1 slice_add_fusion
  255.6 0.6 slice.19
  256.2 0.8 slice.18
  (2 shorter events, 0.1 us)
Async XLA Ops:
  1.6 8.8 %collective-permute-start = (bf16[32,4864]{1,0:T(8,128)(2,1)S(1)}, bf16[32,4864]{1,0:T(8,128)(2,1)S(1)}, u32[]{:S(2)}, u32[]{:S(2)}) collective-permute-start(bf16[32,4864]{1,0:T(8,128)(2,1)S(1)} %pad_maximum_fusion.1), channel_id=1, source_target_pairs={{0,16},{16,0},{32,48},{48,32},{64,80},{80,64},{96,112},{112,96},{1... | collective-permute-start | bytes 933896 | tf_op jit(solution)/shard_map/ppermute | solution.py:415
  3.0 7.5 %copy-start.1 = (bf16[1,1,2,16,4096]{4,3,2,1,0:T(8,128)(2,1)S(1)}, bf16[1,1,2,16,4096]{4,3,2,1,0:T(8,128)(2,1)}, u32[]{:S(2)}) copy-start(bf16[1,1,2,16,4096]{4,3,2,1,0:T(8,128)(2,1)} %param.22) | copy-start | bytes 786436
  3.0 7.5 %copy-start.3 = (bf16[1,1,2,16,768]{4,3,2,1,0:T(8,128)(2,1)S(1)}, bf16[1,1,2,16,768]{4,3,2,1,0:T(8,128)(2,1)}, u32[]{:S(2)}) copy-start(bf16[1,1,2,16,768]{4,3,2,1,0:T(8,128)(2,1)} %param.23) | copy-start | bytes 147460
  10.5 4.6 %copy-start.2 = (bf16[64,4864]{1,0:T(8,128)(2,1)}, bf16[64,4864]{1,0:T(8,128)(2,1)S(1)}, u32[]{:S(2)}) copy-start(bf16[64,4864]{1,0:T(8,128)(2,1)S(1)} %pad_maximum_fusion.refs_0_) | copy-start | bytes 1867780
  10.5 132.4 %collective-permute-start.3 = (bf16[64,4864]{1,0:T(8,128)(2,1)S(1)}, bf16[64,4864]{1,0:T(8,128)(2,1)S(1)}, u32[]{:S(2)}, u32[]{:S(2)}) collective-permute-start(bf16[64,4864]{1,0:T(8,128)(2,1)S(1)} %pad_maximum_fusion.refs_0_), channel_id=1, source_target_pairs={{0,96},{16,112},{32,0},{48,16},{64,32},{80,48},{96,64},{112,80},{1... | collective-permute-start | bytes 1867784 | tf_op jit(solution)/shard_map/ppermute | solution.py:411
  13.4 129.5 %collective-permute-start.2 = (bf16[64,4864]{1,0:T(8,128)(2,1)S(1)}, bf16[64,4864]{1,0:T(8,128)(2,1)S(1)}, u32[]{:S(2)}, u32[]{:S(2)}) collective-permute-start(bf16[64,4864]{1,0:T(8,128)(2,1)S(1)} %pad_maximum_fusion.refs_0_), channel_id=1, source_target_pairs={{0,64},{16,80},{32,96},{48,112},{64,0},{80,16},{96,32},{112,48},{1... | collective-permute-start | bytes 1867784 | tf_op jit(solution)/shard_map/ppermute | solution.py:411
  14.2 128.7 %collective-permute-start.1 = (bf16[64,4864]{1,0:T(8,128)(2,1)S(1)}, bf16[64,4864]{1,0:T(8,128)(2,1)S(1)}, u32[]{:S(2)}, u32[]{:S(2)}) collective-permute-start(bf16[64,4864]{1,0:T(8,128)(2,1)S(1)} %pad_maximum_fusion.refs_0_), channel_id=1, source_target_pairs={{0,32},{16,48},{32,64},{48,80},{64,96},{80,112},{96,0},{112,16},{1... | collective-permute-start | bytes 1867784 | tf_op jit(solution)/shard_map/ppermute | solution.py:411
  142.9 0.9 copy-start.4
  142.9 1.1 copy-start.5
  142.9 1.3 copy-start.6
  178.0 70.2 %collective-permute-start.4 = (f32[64,4864]{1,0:T(8,128)}, f32[64,4864]{1,0:T(8,128)S(1)}, u32[]{:S(2)}, u32[]{:S(2)}) collective-permute-start(f32[64,4864]{1,0:T(8,128)} %get-tuple-element.37), channel_id=1, source_target_pairs={{0,96},{16,112},{32,0},{48,16},{64,32},{80,48},{96,64},{112,80},{1... | collective-permute-start | bytes 3735560 | tf_op jit(solution)/shard_map/ppermute | solution.py:411
  180.5 67.8 %collective-permute-start.5 = (f32[64,4864]{1,0:T(8,128)}, f32[64,4864]{1,0:T(8,128)}, u32[]{:S(2)}, u32[]{:S(2)}) collective-permute-start(f32[64,4864]{1,0:T(8,128)} %get-tuple-element.38), channel_id=1, source_target_pairs={{0,64},{16,80},{32,96},{48,112},{64,0},{80,16},{96,32},{112,48},{1... | collective-permute-start | bytes 3735560 | tf_op jit(solution)/shard_map/ppermute | solution.py:411
  182.0 66.2 %collective-permute-start.6 = (f32[64,4864]{1,0:T(8,128)}, f32[64,4864]{1,0:T(8,128)}, u32[]{:S(2)}, u32[]{:S(2)}) collective-permute-start(f32[64,4864]{1,0:T(8,128)} %get-tuple-element.39), channel_id=1, source_target_pairs={{0,32},{16,48},{32,64},{48,80},{64,96},{80,112},{96,0},{112,16},{1... | collective-permute-start | bytes 3735560 | tf_op jit(solution)/shard_map/ppermute | solution.py:411
  183.3 64.9 %copy-start = (f32[64,4864]{1,0:T(8,128)S(1)}, f32[64,4864]{1,0:T(8,128)}, u32[]{:S(2)}) copy-start(f32[64,4864]{1,0:T(8,128)} %get-tuple-element.41) | copy-start | bytes 3735556
  250.2 5.3 %collective-permute-start.7 = (f32[32,4864]{1,0:T(8,128)S(1)}, f32[32,4864]{1,0:T(8,128)S(1)}, u32[]{:S(2)}, u32[]{:S(2)}) collective-permute-start(f32[32,4864]{1,0:T(8,128)S(1)} %slice.17), channel_id=1, source_target_pairs={{0,16},{16,0},{32,48},{48,32},{64,80},{80,64},{96,112},{112,96},{1... | collective-permute-start | bytes 1867784 | tf_op jit(solution)/shard_map/ppermute | solution.py:415

commit v4 on v3

--- a/solution.py
+++ b/solution.py
@@ -10,6 +10,7 @@
 adapter_scale = 0.5
 LANES = 128
 VMEM_BYTES = 60 * 1024 * 1024
+EXPERT_VMEM_BYTES = 48 * 1024 * 1024
 
 
 def contract_last(left_side, right_side):
@@ -41,6 +42,8 @@
 def dispatch_kernel(
     experts,
     capacity,
+    chips,
+    me_ref,
     idx_ref,
     prob_ref,
     tenant_ref,
@@ -85,7 +88,9 @@
             jnp.sum(jnp.where(m, prob_ref[k : k + 1, :], 0.0), axis=1, keepdims=True)
             for k, m in enumerate(masks)
         )
-        tenant = jnp.sum(filled * tenant_ref[...].astype(jnp.float32), axis=1, keepdims=True)
+        me, owner = me_ref[0], tenant_ref[...]
+        place = lax.rem(me // 2 + chips - lax.div(owner, 2), chips) * 2 + lax.rem(me + owner, 2)
+        tenant = jnp.sum(filled * place.astype(jnp.float32), axis=1, keepdims=True)
         tenant_rows[...] = jnp.broadcast_to(tenant, tenant_rows.shape).astype(jnp.bfloat16)
         tenant_copy.start()
         select[...] = filled.astype(jnp.bfloat16)
@@ -109,15 +114,16 @@
         tenant_copy.wait()
 
 
-def dispatch(idx, prob, tenant, tokens, cotangent, experts, capacity):
+def dispatch(me, idx, prob, tenant, tokens, cotangent, experts, capacity, chips):
     tok_rows, width = tokens.shape
     rows = experts * capacity
     block = 2048
     return pl.pallas_call(
-        functools.partial(dispatch_kernel, experts, capacity),
+        functools.partial(dispatch_kernel, experts, capacity, chips),
         out_shape=jax.ShapeDtypeStruct((rows, 2 * width + LANES), jnp.bfloat16),
         grid=(width // block,),
         in_specs=[
+            pl.BlockSpec(memory_space=pltpu.SMEM),
             pl.BlockSpec(idx.shape, lambda i: (0, 0)),
             pl.BlockSpec(prob.shape, lambda i: (0, 0)),
             pl.BlockSpec(tenant.shape, lambda i: (0, 0)),
@@ -141,7 +147,7 @@
             transcendentals=0,
         ),
         name="dispatch",
-    )(idx, prob, tenant, tokens, cotangent)
+    )(me.reshape(1), idx, prob, tenant, tokens, cotangent)
 
 
 def combine_kernel(experts, capacity, idx_ref, ret_ref, out_ref, select):
@@ -396,7 +402,7 @@
             pltpu.SemaphoreType.DMA((2 * chips,)),
             pltpu.SemaphoreType.DMA((width // 1024,)),
         ],
-        compiler_params=pltpu.CompilerParams(vmem_limit_bytes=VMEM_BYTES),
+        compiler_params=pltpu.CompilerParams(vmem_limit_bytes=EXPERT_VMEM_BYTES),
         cost_estimate=pl.CostEstimate(
             flops=10 * rows * width * hidden + 6 * rows * width * groups,
             bytes_accessed=6 * width * hidden + 6 * rows * width,
@@ -447,12 +453,11 @@
     prob = router_gate_weights.T
     me = lax.axis_index("dp")
     chips = tenants // 2
-    tenant = (me // 2 - token_tenant_index // 2) % chips * 2 + (me + token_tenant_index) % 2
-    tenant = tenant.reshape(1, tok_rows)
+    tenant = token_tenant_index.reshape(1, tok_rows)
     adapters = jnp.concatenate([adapter_down_matrices[0, 0], adapter_up_matrices[0, 0]], axis=-1)
     adapters = adapters.reshape(2 * rank, width + hidden)
     named = me < tenants
-    sent = dispatch(idx, prob, tenant, tokens, cotangent, experts, capacity)
+    sent = dispatch(me, idx, prob, tenant, tokens, cotangent, experts, capacity, chips)
     sent, others = lax.optimization_barrier((sent, other_core(adapters)))
     pair = jnp.concatenate([adapters, others], axis=0)
     held = [pair] + [along_x(pair, step) for step in range(1, chips)]

time: 259 us -> 263 us (1.015)
  local copies, waits for them, and re-layouts: 2.8 us -> 7.25 us
    unnamed x14 -> x16, local copies, waits for them, and re-layouts: 1.28 us -> 5.73 us
where the time goes in v4:
time: 263 us; the launch traced here: 261 us
  blocking collectives  192 us (73%)
  Pallas kernels  47.1 us (18%)
  starting transfers between devices  10 us (4%)
  local copies, waits for them, and re-layouts  7.25 us (3%)
  other arithmetic  3.38 us (1%)
    all_to_all x2, blocking collectives, exchange(): lax.all_to_all(r, 'expert', split_axis=0, concat_axis=0, tiled=True)  192 us
    pallas_call x1, Pallas kernels, expert_pass(): pl.pallas_call(functools.partial(expert_kernel, rank, chips), out_shape=(...  34.5 us
    ppermute x6, starting transfers between devices, along_x(): lax.ppermute(rows, 'dp', [(i, (i + 2 * step) % devices) for i in range(de...  9.87 us
    pallas_call x1, Pallas kernels, dispatch(): pl.pallas_call(functools.partial(dispatch_kernel, experts, capacity, chip...  7.39 us
    unnamed x16, local copies, waits for them, and re-layouts  5.73 us
  transfers between devices with their start and end apart: 8, of which 0 were waited for; matrix products, arithmetic and copies ran while one was open for 0% of the time, Pallas kernels for 5%

profile of v4, /device:TPU:0, one launch (start us, length us, event | category | flops | bytes accessed | tf_op | source)
XLA Modules:
  0.0 261.0 jit_solution(2229152351836568447)
XLA Ops:
  0.6 1.0 pad_maximum_fusion.1
  1.6 0.1 collective-permute-start
  1.7 0.0 copy-start.6
  1.7 0.0 copy-start.7
  1.8 7.4 %dispatch.1 = bf16[640,8320]{1,0:T(8,128)(2,1)} custom-call(s32[1]{0:T(128)} %bitcast.5.me_ref, s32[2,256]{1,0:T(2,128)} %bitcast.25, f32[2,256]{1,0:T(2,128)} %bitcast.27, s32[1,256]{1,0:T(1,128)} %bitcast.28, bf16[256,4096]{1,0:T(8,128)(2,1)} %tok_ref.1, bf16[256,4096]{1,0:T(8,128)(2,1)} %cot_ref.1), custom_call_target="tpu_custom_call" | custom-call | flops 2684354560 | bytes 14680064 | tf_op jit(solution)/shard_map/dispatch/pallas_call | solution.py:121
  9.2 0.0 collective-permute-done
  9.2 0.0 copy-done.6
  9.2 0.0 copy-done.7
  9.2 2.9 %collective-permute-start.3 = (bf16[64,4864]{1,0:T(8,128)(2,1)S(1)}, bf16[64,4864]{1,0:T(8,128)(2,1)S(1)}, u32[]{:S(2)}, u32[]{:S(2)}) collective-permute-start(bf16[64,4864]{1,0:T(8,128)(2,1)S(1)} %pad_maximum_fusion.refs_0_), channel_id=1, source_target_pairs={{0,96},{16,112},{32,0},{48,16},{64,32},{80,48},{96,64},{112,80},{1... | collective-permute-start | bytes 1867784 | tf_op jit(solution)/shard_map/ppermute | solution.py:417
  12.2 0.8 collective-permute-start.2
  13.0 0.9 collective-permute-start.1
  13.8 127.7 %conditional.2 = (bf16[640,8320]{1,0:T(8,128)(2,1)}) conditional(s32[]{:T(128)} %convert_element_type.4, () %tuple.24, bf16[640,8320]{1,0:T(8,128)(2,1)} %dispatch.1), branch_computations={%region_0.0_spmd, %region_1.0_spmd} | conditional | bytes 21299208 | solution.py:425
  13.8 127.7 %all_to_all.18 = bf16[16,40,8320]{2,1,0:T(8,128)(2,1)} all-to-all(bf16[16,40,8320]{2,1,0:T(8,128)(2,1)} %bitcast.15), channel_id=1, replica_groups=mesh['dp'=8,'expert'=16] {'expert'}, dimensions={0} | all-to-all | bytes 21299200 | tf_op jit(solution)/shard_map/cond/branch_1_fun/all_to_all | solution.py:427
  141.6 0.0 collective-permute-done.3.refs_3_
  141.6 0.0 copy-start
  141.6 0.8 copy-done
  142.4 0.0 collective-permute-done.2.refs_2_
  142.4 0.0 copy-start.2
  142.4 0.8 copy-done.2
  143.2 0.0 collective-permute-done.1.refs_1_
  143.3 0.0 copy-start.4
  143.3 0.8 copy-done.4
  144.1 0.0 copy-start.1
  144.1 1.1 copy-done.1
  145.2 0.0 copy-start.3
  145.2 1.1 copy-done.3
  146.2 0.0 copy-start.5
  146.2 1.1 copy-done.5
  147.3 34.5 %expert_pass.1 = (bf16[640,4096]{1,0:T(8,128)(2,1)}, f32[64,4864]{1,0:T(8,128)S(1)}, f32[64,4864]{1,0:T(8,128)}, f32[64,4864]{1,0:T(8,128)S(1)}, f32[64,4864]{1,0:T(8,128)}) custom-call(bf16[640,8320]{1,0:T(8,128)(2,1)} %get-tuple-element.45.got_ref, bf16[4096,768]{1,0:T(8,128)(2,1)} %bitcast.29, bf16[4096,768]{1,0:T(8,128)(2,1)} %bitcast.30, ...), custom_call_target="tpu_custom_call" | custom-call | flops 24159191040 | bytes 34603008 | tf_op jit(solution)/shard_map/expert_pass/pallas_call | solution.py:373
  181.8 2.4 collective-permute-start.4
  184.2 1.5 collective-permute-start.5
  185.8 1.3 collective-permute-start.6
  187.1 64.7 %conditional.3 = (bf16[640,4096]{1,0:T(8,128)(2,1)}) conditional(s32[]{:T(128)} %convert_element_type.4, () %tuple.23, bf16[640,4096]{1,0:T(8,128)(2,1)} %get-tuple-element.35), branch_computations={%region_2.0_spmd, %region_3.0_spmd} | conditional | bytes 10485768 | solution.py:425
  187.1 64.7 %all_to_all.19 = bf16[16,40,4096]{2,1,0:T(8,128)(2,1)} all-to-all(bf16[16,40,4096]{2,1,0:T(8,128)(2,1)} %bitcast.18), channel_id=1, replica_groups=mesh['dp'=8,'expert'=16] {'expert'}, dimensions={0} | all-to-all | bytes 10485760 | tf_op jit(solution)/shard_map/cond/branch_1_fun/all_to_all | solution.py:427
  251.8 0.0 collective-permute-done.4
  251.8 0.0 collective-permute-done.5
  251.8 0.0 collective-permute-done.6
  251.8 2.3 add_add_fusion
  254.2 0.1 collective-permute-start.7
  254.2 5.2 %combine.1 = bf16[256,4096]{1,0:T(8,128)(2,1)} custom-call(s32[2,256]{1,0:T(2,128)} %bitcast.26, bf16[640,4096]{1,0:T(8,128)(2,1)} %get-tuple-element.46.ret_ref), custom_call_target="tpu_custom_call" | custom-call | flops 1342177280 | bytes 7340032 | tf_op jit(solution)/shard_map/combine/pallas_call | solution.py:172
  259.5 0.0 collective-permute-done.7
  259.5 0.1 slice_add_fusion
  259.5 0.6 slice.19
  260.2 0.8 slice.18
  (2 shorter events, 0.1 us)
Async XLA Ops:
  1.6 7.5 %collective-permute-start = (bf16[32,4864]{1,0:T(8,128)(2,1)S(1)}, bf16[32,4864]{1,0:T(8,128)(2,1)S(1)}, u32[]{:S(2)}, u32[]{:S(2)}) collective-permute-start(bf16[32,4864]{1,0:T(8,128)(2,1)S(1)} %pad_maximum_fusion.1), channel_id=1, source_target_pairs={{0,16},{16,0},{32,48},{48,32},{64,80},{80,64},{96,112},{112,96},{1... | collective-permute-start | bytes 933896 | tf_op jit(solution)/shard_map/ppermute | solution.py:421
  1.7 7.4 %copy-start.6 = (bf16[1,1,2,16,4096]{4,3,2,1,0:T(8,128)(2,1)S(1)}, bf16[1,1,2,16,4096]{4,3,2,1,0:T(8,128)(2,1)}, u32[]{:S(2)}) copy-start(bf16[1,1,2,16,4096]{4,3,2,1,0:T(8,128)(2,1)} %param.22) | copy-start | bytes 786436
  1.7 7.4 %copy-start.7 = (bf16[1,1,2,16,768]{4,3,2,1,0:T(8,128)(2,1)S(1)}, bf16[1,1,2,16,768]{4,3,2,1,0:T(8,128)(2,1)}, u32[]{:S(2)}) copy-start(bf16[1,1,2,16,768]{4,3,2,1,0:T(8,128)(2,1)} %param.23) | copy-start | bytes 147460
  9.2 132.3 %collective-permute-start.3 = (bf16[64,4864]{1,0:T(8,128)(2,1)S(1)}, bf16[64,4864]{1,0:T(8,128)(2,1)S(1)}, u32[]{:S(2)}, u32[]{:S(2)}) collective-permute-start(bf16[64,4864]{1,0:T(8,128)(2,1)S(1)} %pad_maximum_fusion.refs_0_), channel_id=1, source_target_pairs={{0,96},{16,112},{32,0},{48,16},{64,32},{80,48},{96,64},{112,80},{1... | collective-permute-start | bytes 1867784 | tf_op jit(solution)/shard_map/ppermute | solution.py:417
  12.2 130.3 %collective-permute-start.2 = (bf16[64,4864]{1,0:T(8,128)(2,1)S(1)}, bf16[64,4864]{1,0:T(8,128)(2,1)S(1)}, u32[]{:S(2)}, u32[]{:S(2)}) collective-permute-start(bf16[64,4864]{1,0:T(8,128)(2,1)S(1)} %pad_maximum_fusion.refs_0_), channel_id=1, source_target_pairs={{0,64},{16,80},{32,96},{48,112},{64,0},{80,16},{96,32},{112,48},{1... | collective-permute-start | bytes 1867784 | tf_op jit(solution)/shard_map/ppermute | solution.py:417
  13.0 130.3 %collective-permute-start.1 = (bf16[64,4864]{1,0:T(8,128)(2,1)S(1)}, bf16[64,4864]{1,0:T(8,128)(2,1)S(1)}, u32[]{:S(2)}, u32[]{:S(2)}) collective-permute-start(bf16[64,4864]{1,0:T(8,128)(2,1)S(1)} %pad_maximum_fusion.refs_0_), channel_id=1, source_target_pairs={{0,32},{16,48},{32,64},{48,80},{64,96},{80,112},{96,0},{112,16},{1... | collective-permute-start | bytes 1867784 | tf_op jit(solution)/shard_map/ppermute | solution.py:417
  141.6 0.8 copy-start
  142.4 0.8 copy-start.2
  143.3 0.8 copy-start.4
  144.1 1.1 copy-start.1
  145.2 1.1 copy-start.3
  146.2 1.1 copy-start.5
  181.8 70.0 %collective-permute-start.4 = (f32[64,4864]{1,0:T(8,128)}, f32[64,4864]{1,0:T(8,128)}, u32[]{:S(2)}, u32[]{:S(2)}) collective-permute-start(f32[64,4864]{1,0:T(8,128)} %get-tuple-element.37), channel_id=1, source_target_pairs={{0,96},{16,112},{32,0},{48,16},{64,32},{80,48},{96,64},{112,80},{1... | collective-permute-start | bytes 3735560 | tf_op jit(solution)/shard_map/ppermute | solution.py:417
  184.2 67.6 %collective-permute-start.5 = (f32[64,4864]{1,0:T(8,128)S(1)}, f32[64,4864]{1,0:T(8,128)}, u32[]{:S(2)}, u32[]{:S(2)}) collective-permute-start(f32[64,4864]{1,0:T(8,128)S(1)} %get-tuple-element.38), channel_id=1, source_target_pairs={{0,64},{16,80},{32,96},{48,112},{64,0},{80,16},{96,32},{112,48},{1... | collective-permute-start | bytes 3735560 | tf_op jit(solution)/shard_map/ppermute | solution.py:417
  185.8 66.1 %collective-permute-start.6 = (f32[64,4864]{1,0:T(8,128)}, f32[64,4864]{1,0:T(8,128)}, u32[]{:S(2)}, u32[]{:S(2)}) collective-permute-start(f32[64,4864]{1,0:T(8,128)} %get-tuple-element.39), channel_id=1, source_target_pairs={{0,32},{16,48},{32,64},{48,80},{64,96},{80,112},{96,0},{112,16},{1... | collective-permute-start | bytes 3735560 | tf_op jit(solution)/shard_map/ppermute | solution.py:417
  254.2 5.3 %collective-permute-start.7 = (f32[32,4864]{1,0:T(8,128)S(1)}, f32[32,4864]{1,0:T(8,128)S(1)}, u32[]{:S(2)}, u32[]{:S(2)}) collective-permute-start(f32[32,4864]{1,0:T(8,128)S(1)} %slice.17), channel_id=1, source_target_pairs={{0,16},{16,0},{32,48},{48,32},{64,80},{80,64},{96,112},{112,96},{1... | collective-permute-start | bytes 1867784 | tf_op jit(solution)/shard_map/ppermute | solution.py:421

commit v5 on v4

--- a/solution.py
+++ b/solution.py
@@ -10,7 +10,7 @@
 adapter_scale = 0.5
 LANES = 128
 VMEM_BYTES = 60 * 1024 * 1024
-EXPERT_VMEM_BYTES = 48 * 1024 * 1024
+EXPERT_VMEM_BYTES = 52 * 1024 * 1024
 
 
 def contract_last(left_side, right_side):

time: 263 us -> 257 us (0.977)
  local copies, waits for them, and re-layouts: 7.25 us -> 2.38 us
    unnamed x16 -> x8, local copies, waits for them, and re-layouts: 5.73 us -> 0.87 us
where the time goes in v5:
time: 257 us; the launch traced here: 255 us
  blocking collectives  193 us (75%)
  Pallas kernels  46.4 us (18%)
  starting transfers between devices  10 us (4%)
  other arithmetic  3 us (1%)
    all_to_all x2, blocking collectives, exchange(): lax.all_to_all(r, 'expert', split_axis=0, concat_axis=0, tiled=True)  193 us
    pallas_call x1, Pallas kernels, expert_pass(): pl.pallas_call(functools.partial(expert_kernel, rank, chips), out_shape=(...  33.8 us
    ppermute x6, starting transfers between devices, along_x(): lax.ppermute(rows, 'dp', [(i, (i + 2 * step) % devices) for i in range(de...  9.85 us
    pallas_call x1, Pallas kernels, dispatch(): pl.pallas_call(functools.partial(dispatch_kernel, experts, capacity, chip...  7.41 us
    pallas_call x1, Pallas kernels, combine(): pl.pallas_call(functools.partial(combine_kernel, experts, capacity), out_...  5.2 us
  transfers between devices with their start and end apart: 8, of which 0 were waited for; matrix products, arithmetic and copies ran while one was open for 0% of the time, Pallas kernels for 5%

profile of v5, /device:TPU:0, one launch (start us, length us, event | category | flops | bytes accessed | tf_op | source)
XLA Modules:
  0.0 255.2 jit_solution(8729378432121111548)
XLA Ops:
  0.6 1.0 pad_maximum_fusion.1
  1.6 0.1 collective-permute-start
  1.7 0.0 copy-start.1
  1.7 0.0 copy-start.2
  1.8 7.4 %dispatch.1 = bf16[640,8320]{1,0:T(8,128)(2,1)} custom-call(s32[1]{0:T(128)} %bitcast.5.me_ref, s32[2,256]{1,0:T(2,128)} %bitcast.25, f32[2,256]{1,0:T(2,128)} %bitcast.27, s32[1,256]{1,0:T(1,128)} %bitcast.28, bf16[256,4096]{1,0:T(8,128)(2,1)} %tok_ref.1, bf16[256,4096]{1,0:T(8,128)(2,1)} %cot_ref.1), custom_call_target="tpu_custom_call" | custom-call | flops 2684354560 | bytes 14680064 | tf_op jit(solution)/shard_map/dispatch/pallas_call | solution.py:121
  9.2 0.0 collective-permute-done
  9.2 0.0 copy-done.1
  9.2 0.0 copy-done.2
  9.3 2.9 %collective-permute-start.3 = (bf16[64,4864]{1,0:T(8,128)(2,1)S(1)}, bf16[64,4864]{1,0:T(8,128)(2,1)S(1)}, u32[]{:S(2)}, u32[]{:S(2)}) collective-permute-start(bf16[64,4864]{1,0:T(8,128)(2,1)S(1)} %pad_maximum_fusion.refs_0_), channel_id=1, source_target_pairs={{0,96},{16,112},{32,0},{48,16},{64,32},{80,48},{96,64},{112,80},{1... | collective-permute-start | bytes 1867784 | tf_op jit(solution)/shard_map/ppermute | solution.py:417
  12.2 0.8 collective-permute-start.2
  13.0 0.9 collective-permute-start.1
  13.9 127.7 %conditional.2 = (bf16[640,8320]{1,0:T(8,128)(2,1)}) conditional(s32[]{:T(128)} %convert_element_type.4, () %tuple.24, bf16[640,8320]{1,0:T(8,128)(2,1)} %dispatch.1), branch_computations={%region_0.0_spmd, %region_1.0_spmd} | conditional | bytes 21299208 | solution.py:425
  13.9 127.7 %all_to_all.18 = bf16[16,40,8320]{2,1,0:T(8,128)(2,1)} all-to-all(bf16[16,40,8320]{2,1,0:T(8,128)(2,1)} %bitcast.15), channel_id=1, replica_groups=mesh['dp'=8,'expert'=16] {'expert'}, dimensions={0} | all-to-all | bytes 21299200 | tf_op jit(solution)/shard_map/cond/branch_1_fun/all_to_all | solution.py:427
  141.6 0.0 collective-permute-done.3.refs_3_
  141.6 0.0 copy-start.3
  141.6 0.0 collective-permute-done.2.refs_2_
  141.6 0.0 collective-permute-done.1.refs_1_
  141.6 0.8 copy-done.3
  142.5 33.8 %expert_pass.1 = (bf16[640,4096]{1,0:T(8,128)(2,1)}, f32[64,4864]{1,0:T(8,128)}, f32[64,4864]{1,0:T(8,128)}, f32[64,4864]{1,0:T(8,128)}, f32[64,4864]{1,0:T(8,128)}) custom-call(bf16[640,8320]{1,0:T(8,128)(2,1)} %get-tuple-element.45.got_ref, bf16[4096,768]{1,0:T(8,128)(2,1)} %bitcast.29, bf16[4096,768]{1,0:T(8,128)(2,1)} %bitcast.30, ...), custom_call_target="tpu_custom_call" | custom-call | flops 24159191040 | bytes 34603008 | tf_op jit(solution)/shard_map/expert_pass/pallas_call | solution.py:373
  176.2 2.4 collective-permute-start.4
  178.7 1.5 collective-permute-start.5
  180.2 1.3 collective-permute-start.6
  181.5 0.0 copy-start
  181.5 64.9 %conditional.3 = (bf16[640,4096]{1,0:T(8,128)(2,1)}) conditional(s32[]{:T(128)} %convert_element_type.4, () %tuple.23, bf16[640,4096]{1,0:T(8,128)(2,1)} %get-tuple-element.35), branch_computations={%region_2.0_spmd, %region_3.0_spmd} | conditional | bytes 10485768 | solution.py:425
  181.5 64.9 %all_to_all.19 = bf16[16,40,4096]{2,1,0:T(8,128)(2,1)} all-to-all(bf16[16,40,4096]{2,1,0:T(8,128)(2,1)} %bitcast.18), channel_id=1, replica_groups=mesh['dp'=8,'expert'=16] {'expert'}, dimensions={0} | all-to-all | bytes 10485760 | tf_op jit(solution)/shard_map/cond/branch_1_fun/all_to_all | solution.py:427
  246.4 0.0 collective-permute-done.4
  246.4 0.0 collective-permute-done.5
  246.4 0.0 collective-permute-done.6
  246.4 0.0 copy-done
  246.4 1.9 add_add_fusion
  248.4 0.1 collective-permute-start.7
  248.5 5.2 %combine.1 = bf16[256,4096]{1,0:T(8,128)(2,1)} custom-call(s32[2,256]{1,0:T(2,128)} %bitcast.26, bf16[640,4096]{1,0:T(8,128)(2,1)} %get-tuple-element.46.ret_ref), custom_call_target="tpu_custom_call" | custom-call | flops 1342177280 | bytes 7340032 | tf_op jit(solution)/shard_map/combine/pallas_call | solution.py:172
  253.7 0.0 collective-permute-done.7
  253.7 0.1 slice_add_fusion
  253.7 0.6 slice.19
  254.4 0.8 slice.18
  (2 shorter events, 0.1 us)
Async XLA Ops:
  1.6 7.5 %collective-permute-start = (bf16[32,4864]{1,0:T(8,128)(2,1)S(1)}, bf16[32,4864]{1,0:T(8,128)(2,1)S(1)}, u32[]{:S(2)}, u32[]{:S(2)}) collective-permute-start(bf16[32,4864]{1,0:T(8,128)(2,1)S(1)} %pad_maximum_fusion.1), channel_id=1, source_target_pairs={{0,16},{16,0},{32,48},{48,32},{64,80},{80,64},{96,112},{112,96},{1... | collective-permute-start | bytes 933896 | tf_op jit(solution)/shard_map/ppermute | solution.py:421
  1.7 7.5 %copy-start.1 = (bf16[1,1,2,16,4096]{4,3,2,1,0:T(8,128)(2,1)S(1)}, bf16[1,1,2,16,4096]{4,3,2,1,0:T(8,128)(2,1)}, u32[]{:S(2)}) copy-start(bf16[1,1,2,16,4096]{4,3,2,1,0:T(8,128)(2,1)} %param.22) | copy-start | bytes 786436
  1.7 7.5 %copy-start.2 = (bf16[1,1,2,16,768]{4,3,2,1,0:T(8,128)(2,1)S(1)}, bf16[1,1,2,16,768]{4,3,2,1,0:T(8,128)(2,1)}, u32[]{:S(2)}) copy-start(bf16[1,1,2,16,768]{4,3,2,1,0:T(8,128)(2,1)} %param.23) | copy-start | bytes 147460
  9.3 132.3 %collective-permute-start.3 = (bf16[64,4864]{1,0:T(8,128)(2,1)S(1)}, bf16[64,4864]{1,0:T(8,128)(2,1)S(1)}, u32[]{:S(2)}, u32[]{:S(2)}) collective-permute-start(bf16[64,4864]{1,0:T(8,128)(2,1)S(1)} %pad_maximum_fusion.refs_0_), channel_id=1, source_target_pairs={{0,96},{16,112},{32,0},{48,16},{64,32},{80,48},{96,64},{112,80},{1... | collective-permute-start | bytes 1867784 | tf_op jit(solution)/shard_map/ppermute | solution.py:417
  12.2 129.4 %collective-permute-start.2 = (bf16[64,4864]{1,0:T(8,128)(2,1)S(1)}, bf16[64,4864]{1,0:T(8,128)(2,1)S(1)}, u32[]{:S(2)}, u32[]{:S(2)}) collective-permute-start(bf16[64,4864]{1,0:T(8,128)(2,1)S(1)} %pad_maximum_fusion.refs_0_), channel_id=1, source_target_pairs={{0,64},{16,80},{32,96},{48,112},{64,0},{80,16},{96,32},{112,48},{1... | collective-permute-start | bytes 1867784 | tf_op jit(solution)/shard_map/ppermute | solution.py:417
  13.0 128.6 %collective-permute-start.1 = (bf16[64,4864]{1,0:T(8,128)(2,1)S(1)}, bf16[64,4864]{1,0:T(8,128)(2,1)S(1)}, u32[]{:S(2)}, u32[]{:S(2)}) collective-permute-start(bf16[64,4864]{1,0:T(8,128)(2,1)S(1)} %pad_maximum_fusion.refs_0_), channel_id=1, source_target_pairs={{0,32},{16,48},{32,64},{48,80},{64,96},{80,112},{96,0},{112,16},{1... | collective-permute-start | bytes 1867784 | tf_op jit(solution)/shard_map/ppermute | solution.py:417
  141.6 0.9 copy-start.3
  176.2 70.2 %collective-permute-start.4 = (f32[64,4864]{1,0:T(8,128)}, f32[64,4864]{1,0:T(8,128)S(1)}, u32[]{:S(2)}, u32[]{:S(2)}) collective-permute-start(f32[64,4864]{1,0:T(8,128)} %get-tuple-element.37), channel_id=1, source_target_pairs={{0,96},{16,112},{32,0},{48,16},{64,32},{80,48},{96,64},{112,80},{1... | collective-permute-start | bytes 3735560 | tf_op jit(solution)/shard_map/ppermute | solution.py:417
  178.7 67.8 %collective-permute-start.5 = (f32[64,4864]{1,0:T(8,128)}, f32[64,4864]{1,0:T(8,128)}, u32[]{:S(2)}, u32[]{:S(2)}) collective-permute-start(f32[64,4864]{1,0:T(8,128)} %get-tuple-element.38), channel_id=1, source_target_pairs={{0,64},{16,80},{32,96},{48,112},{64,0},{80,16},{96,32},{112,48},{1... | collective-permute-start | bytes 3735560 | tf_op jit(solution)/shard_map/ppermute | solution.py:417
  180.2 66.2 %collective-permute-start.6 = (f32[64,4864]{1,0:T(8,128)}, f32[64,4864]{1,0:T(8,128)}, u32[]{:S(2)}, u32[]{:S(2)}) collective-permute-start(f32[64,4864]{1,0:T(8,128)} %get-tuple-element.39), channel_id=1, source_target_pairs={{0,32},{16,48},{32,64},{48,80},{64,96},{80,112},{96,0},{112,16},{1... | collective-permute-start | bytes 3735560 | tf_op jit(solution)/shard_map/ppermute | solution.py:417
  181.5 64.9 %copy-start = (f32[64,4864]{1,0:T(8,128)S(1)}, f32[64,4864]{1,0:T(8,128)}, u32[]{:S(2)}) copy-start(f32[64,4864]{1,0:T(8,128)} %get-tuple-element.41) | copy-start | bytes 3735556
  248.4 5.3 %collective-permute-start.7 = (f32[32,4864]{1,0:T(8,128)S(1)}, f32[32,4864]{1,0:T(8,128)S(1)}, u32[]{:S(2)}, u32[]{:S(2)}) collective-permute-start(f32[32,4864]{1,0:T(8,128)S(1)} %slice.17), channel_id=1, source_target_pairs={{0,16},{16,0},{32,48},{48,32},{64,80},{80,64},{96,112},{112,96},{1... | collective-permute-start | bytes 1867784 | tf_op jit(solution)/shard_map/ppermute | solution.py:421

commit v6 on v5

--- a/solution.py
+++ b/solution.py
@@ -475,8 +475,9 @@
     returned = exchange(named, route_grad)
     returned, own, *arrived = lax.optimization_barrier((returned, own, *arrived))
     token_grads = combine(idx, returned, experts, capacity)
-    total = sum(arrived, own)
-    owned = total[: 2 * rank] + other_core(total[2 * rank :])
+    theirs = sum((part[2 * rank :] for part in arrived), own[2 * rank :])
+    mine = sum((part[: 2 * rank] for part in arrived), own[: 2 * rank])
+    owned = mine + other_core(theirs)
     down_owned = owned[:, :width].reshape(1, 1, 2, rank, width)
     up_owned = owned[:, width:].reshape(1, 1, 2, rank, hidden)
     return token_grads, down_owned, up_owned

time: 257 us -> 258 us (level)
  no operation moved by 1% of the time
where the time goes in v6:
time: 258 us; the launch traced here: 257 us
  blocking collectives  193 us (75%)
  Pallas kernels  46.4 us (18%)
  starting transfers between devices  9.94 us (4%)
  other arithmetic  4.67 us (2%)
    all_to_all x2, blocking collectives, exchange(): lax.all_to_all(r, 'expert', split_axis=0, concat_axis=0, tiled=True)  193 us
    pallas_call x1, Pallas kernels, expert_pass(): pl.pallas_call(functools.partial(expert_kernel, rank, chips), out_shape=(...  33.8 us
    ppermute x6, starting transfers between devices, along_x(): lax.ppermute(rows, 'dp', [(i, (i + 2 * step) % devices) for i in range(de...  9.85 us
    pallas_call x1, Pallas kernels, dispatch(): pl.pallas_call(functools.partial(dispatch_kernel, experts, capacity, chip...  7.41 us
    pallas_call x1, Pallas kernels, combine(): pl.pallas_call(functools.partial(combine_kernel, experts, capacity), out_...  5.19 us
  transfers between devices with their start and end apart: 8, of which 0 were waited for; matrix products, arithmetic and copies ran while one was open for 0% of the time, Pallas kernels for 5%

profile of v6, /device:TPU:0, one launch (start us, length us, event | category | flops | bytes accessed | tf_op | source)
XLA Modules:
  0.0 256.7 jit_solution(1932547882417508837)
XLA Ops:
  0.6 1.0 pad_maximum_fusion.1
  1.6 0.1 collective-permute-start
  1.7 0.0 copy-start.1
  1.7 0.0 copy-start.2
  1.8 7.4 %dispatch.1 = bf16[640,8320]{1,0:T(8,128)(2,1)} custom-call(s32[1]{0:T(128)} %bitcast.5.me_ref, s32[2,256]{1,0:T(2,128)} %bitcast.25, f32[2,256]{1,0:T(2,128)} %bitcast.27, s32[1,256]{1,0:T(1,128)} %bitcast.28, bf16[256,4096]{1,0:T(8,128)(2,1)} %tok_ref.1, bf16[256,4096]{1,0:T(8,128)(2,1)} %cot_ref.1), custom_call_target="tpu_custom_call" | custom-call | flops 2684354560 | bytes 14680064 | tf_op jit(solution)/shard_map/dispatch/pallas_call | solution.py:121
  9.2 0.0 collective-permute-done
  9.2 0.0 copy-done.1
  9.2 0.0 copy-done.2
  9.3 2.9 %collective-permute-start.3 = (bf16[64,4864]{1,0:T(8,128)(2,1)S(1)}, bf16[64,4864]{1,0:T(8,128)(2,1)S(1)}, u32[]{:S(2)}, u32[]{:S(2)}) collective-permute-start(bf16[64,4864]{1,0:T(8,128)(2,1)S(1)} %pad_maximum_fusion.refs_0_), channel_id=1, source_target_pairs={{0,96},{16,112},{32,0},{48,16},{64,32},{80,48},{96,64},{112,80},{1... | collective-permute-start | bytes 1867784 | tf_op jit(solution)/shard_map/ppermute | solution.py:417
  12.2 0.8 collective-permute-start.2
  13.0 0.9 collective-permute-start.1
  13.9 127.7 %conditional.2 = (bf16[640,8320]{1,0:T(8,128)(2,1)}) conditional(s32[]{:T(128)} %convert_element_type.4, () %tuple.24, bf16[640,8320]{1,0:T(8,128)(2,1)} %dispatch.1), branch_computations={%region_0.0_spmd, %region_1.0_spmd} | conditional | bytes 21299208 | solution.py:425
  13.9 127.7 %all_to_all.18 = bf16[16,40,8320]{2,1,0:T(8,128)(2,1)} all-to-all(bf16[16,40,8320]{2,1,0:T(8,128)(2,1)} %bitcast.15), channel_id=1, replica_groups=mesh['dp'=8,'expert'=16] {'expert'}, dimensions={0} | all-to-all | bytes 21299200 | tf_op jit(solution)/shard_map/cond/branch_1_fun/all_to_all | solution.py:427
  141.6 0.0 collective-permute-done.3.refs_3_
  141.6 0.0 copy-start.3
  141.6 0.0 collective-permute-done.2.refs_2_
  141.6 0.0 collective-permute-done.1.refs_1_
  141.6 0.8 copy-done.3
  142.4 33.8 %expert_pass.1 = (bf16[640,4096]{1,0:T(8,128)(2,1)}, f32[64,4864]{1,0:T(8,128)}, f32[64,4864]{1,0:T(8,128)}, f32[64,4864]{1,0:T(8,128)}, f32[64,4864]{1,0:T(8,128)}) custom-call(bf16[640,8320]{1,0:T(8,128)(2,1)} %get-tuple-element.45.got_ref, bf16[4096,768]{1,0:T(8,128)(2,1)} %bitcast.29, bf16[4096,768]{1,0:T(8,128)(2,1)} %bitcast.30, ...), custom_call_target="tpu_custom_call" | custom-call | flops 24159191040 | bytes 34603008 | tf_op jit(solution)/shard_map/expert_pass/pallas_call | solution.py:373
  176.2 2.4 collective-permute-start.4
  178.6 1.5 collective-permute-start.5
  180.1 1.3 collective-permute-start.6
  181.5 0.0 copy-start
  181.5 64.9 %conditional.3 = (bf16[640,4096]{1,0:T(8,128)(2,1)}) conditional(s32[]{:T(128)} %convert_element_type.4, () %tuple.23, bf16[640,4096]{1,0:T(8,128)(2,1)} %get-tuple-element.35), branch_computations={%region_2.0_spmd, %region_3.0_spmd} | conditional | bytes 10485768 | solution.py:425
  181.5 64.9 %all_to_all.19 = bf16[16,40,4096]{2,1,0:T(8,128)(2,1)} all-to-all(bf16[16,40,4096]{2,1,0:T(8,128)(2,1)} %bitcast.18), channel_id=1, replica_groups=mesh['dp'=8,'expert'=16] {'expert'}, dimensions={0} | all-to-all | bytes 10485760 | tf_op jit(solution)/shard_map/cond/branch_1_fun/all_to_all | solution.py:427
  246.3 0.0 collective-permute-done.4
  246.3 0.0 collective-permute-done.5
  246.3 0.0 collective-permute-done.6
  246.4 0.0 copy-done
  246.4 2.2 slice_add_fusion
  248.6 0.0 collective-permute-start.7
  248.6 5.2 %combine.1 = bf16[256,4096]{1,0:T(8,128)(2,1)} custom-call(s32[2,256]{1,0:T(2,128)} %bitcast.26, bf16[640,4096]{1,0:T(8,128)(2,1)} %get-tuple-element.46.ret_ref), custom_call_target="tpu_custom_call" | custom-call | flops 1342177280 | bytes 7340032 | tf_op jit(solution)/shard_map/combine/pallas_call | solution.py:172
  253.8 0.0 collective-permute-done.7
  253.8 1.4 add_add_fusion
  255.2 0.6 slice.41
  255.8 0.8 slice.40
  (1 shorter events, 0.0 us)
Async XLA Ops:
  1.6 7.5 %collective-permute-start = (bf16[32,4864]{1,0:T(8,128)(2,1)S(1)}, bf16[32,4864]{1,0:T(8,128)(2,1)S(1)}, u32[]{:S(2)}, u32[]{:S(2)}) collective-permute-start(bf16[32,4864]{1,0:T(8,128)(2,1)S(1)} %pad_maximum_fusion.1), channel_id=1, source_target_pairs={{0,16},{16,0},{32,48},{48,32},{64,80},{80,64},{96,112},{112,96},{1... | collective-permute-start | bytes 933896 | tf_op jit(solution)/shard_map/ppermute | solution.py:421
  1.7 7.5 %copy-start.1 = (bf16[1,1,2,16,4096]{4,3,2,1,0:T(8,128)(2,1)S(1)}, bf16[1,1,2,16,4096]{4,3,2,1,0:T(8,128)(2,1)}, u32[]{:S(2)}) copy-start(bf16[1,1,2,16,4096]{4,3,2,1,0:T(8,128)(2,1)} %param.22) | copy-start | bytes 786436
  1.7 7.5 %copy-start.2 = (bf16[1,1,2,16,768]{4,3,2,1,0:T(8,128)(2,1)S(1)}, bf16[1,1,2,16,768]{4,3,2,1,0:T(8,128)(2,1)}, u32[]{:S(2)}) copy-start(bf16[1,1,2,16,768]{4,3,2,1,0:T(8,128)(2,1)} %param.23) | copy-start | bytes 147460
  9.3 132.3 %collective-permute-start.3 = (bf16[64,4864]{1,0:T(8,128)(2,1)S(1)}, bf16[64,4864]{1,0:T(8,128)(2,1)S(1)}, u32[]{:S(2)}, u32[]{:S(2)}) collective-permute-start(bf16[64,4864]{1,0:T(8,128)(2,1)S(1)} %pad_maximum_fusion.refs_0_), channel_id=1, source_target_pairs={{0,96},{16,112},{32,0},{48,16},{64,32},{80,48},{96,64},{112,80},{1... | collective-permute-start | bytes 1867784 | tf_op jit(solution)/shard_map/ppermute | solution.py:417
  12.2 129.4 %collective-permute-start.2 = (bf16[64,4864]{1,0:T(8,128)(2,1)S(1)}, bf16[64,4864]{1,0:T(8,128)(2,1)S(1)}, u32[]{:S(2)}, u32[]{:S(2)}) collective-permute-start(bf16[64,4864]{1,0:T(8,128)(2,1)S(1)} %pad_maximum_fusion.refs_0_), channel_id=1, source_target_pairs={{0,64},{16,80},{32,96},{48,112},{64,0},{80,16},{96,32},{112,48},{1... | collective-permute-start | bytes 1867784 | tf_op jit(solution)/shard_map/ppermute | solution.py:417
  13.0 128.6 %collective-permute-start.1 = (bf16[64,4864]{1,0:T(8,128)(2,1)S(1)}, bf16[64,4864]{1,0:T(8,128)(2,1)S(1)}, u32[]{:S(2)}, u32[]{:S(2)}) collective-permute-start(bf16[64,4864]{1,0:T(8,128)(2,1)S(1)} %pad_maximum_fusion.refs_0_), channel_id=1, source_target_pairs={{0,32},{16,48},{32,64},{48,80},{64,96},{80,112},{96,0},{112,16},{1... | collective-permute-start | bytes 1867784 | tf_op jit(solution)/shard_map/ppermute | solution.py:417
  141.6 0.8 copy-start.3
  176.2 70.1 %collective-permute-start.4 = (f32[64,4864]{1,0:T(8,128)}, f32[64,4864]{1,0:T(8,128)S(1)}, u32[]{:S(2)}, u32[]{:S(2)}) collective-permute-start(f32[64,4864]{1,0:T(8,128)} %get-tuple-element.37), channel_id=1, source_target_pairs={{0,96},{16,112},{32,0},{48,16},{64,32},{80,48},{96,64},{112,80},{1... | collective-permute-start | bytes 3735560 | tf_op jit(solution)/shard_map/ppermute | solution.py:417
  178.6 67.7 %collective-permute-start.5 = (f32[64,4864]{1,0:T(8,128)}, f32[64,4864]{1,0:T(8,128)}, u32[]{:S(2)}, u32[]{:S(2)}) collective-permute-start(f32[64,4864]{1,0:T(8,128)} %get-tuple-element.38), channel_id=1, source_target_pairs={{0,64},{16,80},{32,96},{48,112},{64,0},{80,16},{96,32},{112,48},{1... | collective-permute-start | bytes 3735560 | tf_op jit(solution)/shard_map/ppermute | solution.py:417
  180.1 66.2 %collective-permute-start.6 = (f32[64,4864]{1,0:T(8,128)}, f32[64,4864]{1,0:T(8,128)}, u32[]{:S(2)}, u32[]{:S(2)}) collective-permute-start(f32[64,4864]{1,0:T(8,128)} %get-tuple-element.39), channel_id=1, source_target_pairs={{0,32},{16,48},{32,64},{48,80},{64,96},{80,112},{96,0},{112,16},{1... | collective-permute-start | bytes 3735560 | tf_op jit(solution)/shard_map/ppermute | solution.py:417
  181.5 64.9 %copy-start = (f32[64,4864]{1,0:T(8,128)S(1)}, f32[64,4864]{1,0:T(8,128)}, u32[]{:S(2)}) copy-start(f32[64,4864]{1,0:T(8,128)} %get-tuple-element.41) | copy-start | bytes 3735556
  248.6 5.2 %collective-permute-start.7 = (f32[32,4864]{1,0:T(8,128)}, f32[32,4864]{1,0:T(8,128)S(1)}, u32[]{:S(2)}, u32[]{:S(2)}) collective-permute-start(f32[32,4864]{1,0:T(8,128)} %slice_add_fusion), channel_id=1, source_target_pairs={{0,16},{16,0},{32,48},{48,32},{64,80},{80,64},{96,112},{112,96},{1... | collective-permute-start | bytes 1867784 | tf_op jit(solution)/shard_map/ppermute | solution.py:421
